TPU v7x, 32 devices: a whole 2x2x4 slice. The times are simulated.
32 devices in a mesh: wide: 8 (over y, x, core), grp: 4 (over z).
Axes of the slice: x: 2, y: 2, z: 4, core: 2. Of those that a mesh axis runs over, the one named last changes fastest.
Arguments:
- source: float32 [64, 64, 128], P('wide', 'grp'), may hold values from -6 to 6
- conductivity: float32 [64, 64, 128], P('wide', 'grp'), may hold values from 0.02 to 0.5
- ice_cells: int32 [64, 64], P('wide', 'grp'), may hold values from 1 to 128, as said below
Outputs:
- pressure: float32 [64, 64, 128], P('wide', 'grp')
Inputs may be any that keep to these rules, and one draw needn't show every extreme that they name: Column (x, y) holds ice in its lowest ice_cells[x, y] cells; some column is 128 cells high.
All inputs are finite; a program needn't handle non-finite values.
Results may differ from a plain program's by a relative error of at most 0.0001.
Values sent between devices are 32-bit elements; how exact they have to be, the bound alone decides.
A program may use at most 64 MiB of HBM per device.

v0:
```python
import jax
import jax.numpy as jnp
from jax import lax
from jax.sharding import PartitionSpec as P

ITERS = 6


cheb_center = (2.0 + 0.3) / 2.0
cheb_radius = (2.0 - 0.3) / 2.0
first_ratio = cheb_radius / cheb_center
second_ratio = 1.0 / (2.0 * cheb_center / cheb_radius - first_ratio)
carry_weight = second_ratio * first_ratio
fresh_weight = 2.0 * second_ratio / cheb_radius


def with_halo(value, sides, width):
    for axis, dim in sides:
        peers, length = (lax.axis_size(axis), value.shape[dim])
        up = [(i, (i + 1) % peers) for i in range(peers - 1)]
        down = [(j, i) for i, j in up]
        last = lax.slice_in_dim(value, length - width, length, axis=dim)
        initial = lax.slice_in_dim(value, 0, width, axis=dim)
        before = lax.ppermute(last, axis, up)
        after = lax.ppermute(initial, axis, down)
        value = jnp.concatenate([before, value, after], axis=dim)
    return value


def rim_both(values):
    return with_halo(values, (("wide", 0), ("grp", 1)), 1)


def rim_wide(values):
    widened = with_halo(values, (("wide", 0),), 1)
    border = jnp.zeros((widened.shape[0], 1, widened.shape[2]), widened.dtype)
    return jnp.concatenate([border, widened, border], 1)


def sum_wide(partial_sum):
    return lax.psum(partial_sum, "wide")


def agglomerate(source_term, coef_field, heights):
    return (
        lax.all_gather(source_term, "grp", axis=1, tiled=True),
        lax.all_gather(coef_field, "grp", axis=1, tiled=True),
        lax.all_gather(heights, "grp", axis=1, tiled=True),
    )


def beside_all(padded, values, above):
    below = jnp.zeros_like(above)
    return (
        padded[2:, 1:-1],
        padded[:-2, 1:-1],
        padded[1:-1, 2:],
        padded[1:-1, :-2],
        jnp.concatenate([values[:, :, 1:], above], 2),
        jnp.concatenate([below, values[:, :, :-1]], 2),
    )


def level_setup(coef_field, heights, coarsening, widener):
    factor = float(2**coarsening)
    others = beside_all(widener(coef_field), coef_field, coef_field[:, :, -1:])
    weights = tuple(
        (factor * 2.0 * coef_field * neighbour / (coef_field + neighbour) for neighbour in others)
    )
    diagonal = weights[0]
    for weight in weights[1:]:
        diagonal = diagonal + weight
    layers = jnp.arange(coef_field.shape[2], dtype=jnp.float32) * factor
    active = (layers[None, None, :] < heights[:, :, None]).astype(jnp.float32)
    return (weights, diagonal, active)


def operate(values, setup, widener):
    weights, diagonal, active = setup
    others = beside_all(widener(values), values, jnp.zeros_like(values[:, :, :1]))
    coupled = weights[0] * others[0]
    for weight, neighbour in zip(weights[1:], others[1:]):
        coupled = coupled + weight * neighbour
    return active * (diagonal * values - coupled)


def smooth(guess, source_term, setup, widener, fresh):
    diagonal = setup[1]
    if fresh:
        residual = source_term
    else:
        residual = source_term - operate(guess, setup, widener)
    update = residual / (cheb_center * diagonal)
    guess = update if fresh else guess + update
    residual = source_term - operate(guess, setup, widener)
    update = carry_weight * update + fresh_weight * residual / diagonal
    return guess + update


def children_sum(values):
    extent_x, extent_y, extent_z = values.shape
    return values.reshape(extent_x // 2, 2, extent_y // 2, 2, extent_z // 2, 2).sum(axis=(1, 3, 5))


def column_top(heights):
    extent_x, extent_y = heights.shape
    return heights.reshape(extent_x // 2, 2, extent_y // 2, 2).max(axis=(1, 3))


def spread_children(values):
    return jnp.repeat(jnp.repeat(jnp.repeat(values, 2, 0), 2, 1), 2, 2)


def conjugate(source_term, setup, widener, reduce_all):
    solution = jnp.zeros_like(source_term)
    residual = source_term
    direction = source_term
    current = reduce_all(jnp.sum(residual * residual))
    for iteration in range(ITERS):
        applied = operate(direction, setup, widener)
        step_size = current / reduce_all(jnp.sum(direction * applied))
        solution = solution + step_size * direction
        residual = residual - step_size * applied
        following = reduce_all(jnp.sum(residual * residual))
        direction = residual + following / current * direction
        current = following
    return solution


def own_part(strip_values, own_width):
    group_index = lax.axis_index("grp")
    return lax.dynamic_slice_in_dim(strip_values, group_index * own_width, own_width, 1)


def middle(source_term, coef_field, heights, widener, coarse_solve):
    setup = level_setup(coef_field, heights, 1, widener)
    smoothed = smooth(jnp.zeros_like(source_term), source_term, setup, widener, True)
    lower_term = children_sum(source_term - operate(smoothed, setup, widener))
    correction = coarse_solve(lower_term, children_sum(coef_field) * 0.125, column_top(heights))
    smoothed = smoothed + setup[2] * spread_children(correction)
    return smooth(smoothed, source_term, setup, widener, False)


def strip_lower(lower_term, coef_field, heights):
    setup = level_setup(coef_field, heights, 2, rim_wide)
    return conjugate(lower_term, setup, rim_wide, sum_wide)


def shards(source, conductivity, ice_cells):
    heights = ice_cells.astype(jnp.float32)
    setup = level_setup(conductivity, heights, 0, rim_both)
    source_term = setup[2] * source
    smoothed = smooth(jnp.zeros_like(source_term), source_term, setup, rim_both, True)
    lower_term = children_sum(source_term - operate(smoothed, setup, rim_both))
    lower_coef = children_sum(conductivity) * 0.125
    lower_heights = column_top(heights)
    own_width = lower_term.shape[1]
    strip_term, strip_coef, strip_heights = agglomerate(lower_term, lower_coef, lower_heights)
    correction = own_part(
        middle(strip_term, strip_coef, strip_heights, rim_wide, strip_lower), own_width
    )
    smoothed = smoothed + setup[2] * spread_children(correction)
    return smooth(smoothed, source_term, setup, rim_both, False)


def solution(mesh):
    placed = (P("wide", "grp", None), P("wide", "grp", None), P("wide", "grp"))
    return jax.shard_map(
        shards, mesh=mesh, in_specs=placed, out_specs=P("wide", "grp", None), check_vma=False
    )
```

profile of v0, /device:TPU:28, one launch (start us, length us, event | category | flops | bytes accessed | tf_op | source)
XLA Modules:
  0.0 389.3 jit_solution(13858575206703795755)
XLA Ops:
  2.6 4.5 %collective-permute-start = (f32[1,16,128]{2,1,0:T(8,128)S(1)}, f32[1,16,128]{2,1,0:T(8,128)S(1)}, u32[]{:S(2)}, u32[]{:S(2)}) collective-permute-start(f32[1,16,128]{2,1,0:T(8,128)S(1)} %get-tuple-element.95), channel_id=1, source_target_pairs={{4,0},{8,4},{12,8},{16,12},{20,16},{24,20},{28,24},{5,1},{9,5},{13... | collective-permute-start | bytes 24584 | tf_op jit(solution)/shard_map/ppermute | solution.py:25
  7.2 6.3 %reshape.48 = f32[4,2,8,2,64,2]{5,4,3,2,1,0:T(8,128)} reshape(f32[8,16,128]{2,1,0:T(8,128)} %param.4) | data formatting | bytes 131072 | tf_op jit(solution)/shard_map/reshape | solution.py:102
  13.5 2.6 reduce_sum.145
  16.1 13.1 %all_gather.10 = f32[4,32,64]{2,0,1:T(4,128)S(1)} all-gather(f32[4,8,64]{2,0,1:T(4,128)S(1)} %copy.141), channel_id=1, replica_groups=mesh['wide'=8,'grp'=4] {'grp'}, dimensions={1}, use_global_device_ids=true | all-gather | bytes 40960 | tf_op jit(solution)/shard_map/all_gather | solution.py:47
  33.6 4.5 %collective-permute-start.18 = (f32[1,16,32]{2,1,0:T(8,128)S(1)}, f32[1,16,32]{2,1,0:T(8,128)S(1)}, u32[]{:S(2)}, u32[]{:S(2)}) collective-permute-start(f32[1,16,32]{2,1,0:T(8,128)S(1)} %get-tuple-element.117), channel_id=1, source_target_pairs={{4,0},{8,4},{12,8},{16,12},{20,16},{24,20},{28,24},{5,1},{9,5},{13... | collective-permute-start | bytes 6152 | tf_op jit(solution)/shard_map/ppermute | solution.py:25
  40.5 10.6 %all-gather = f32[4,8,4]{1,2,0:T(4,128)S(1)} all-gather(f32[1,8,4]{1,2,0:T(4,128)S(1)} %bitcast.24), channel_id=1, replica_groups=mesh['wide'=8,'grp'=4] {'grp'}, dimensions={0}, use_global_device_ids=true | all-gather | bytes 640 | tf_op jit(solution)/shard_map/all_gather | solution.py:48
  57.3 4.3 %collective-permute-done.3 = f32[10,1,128]{2,1,0:T(1,128)S(1)} collective-permute-done((f32[10,1,128]{2,1,0:T(1,128)S(1)}, f32[10,1,128]{2,1,0:T(1,128)S(1)}, u32[]{:S(2)}, u32[]{:S(2)}) %collective-permute-start.3) | collective-permute-done | bytes 5152 | tf_op jit(solution)/shard_map/ppermute | solution.py:24
  63.6 2.4 collective-permute-start.5
  66.1 3.4 collective-permute-done.5
  69.5 3.9 %collective-permute-start.6 = (f32[10,1,128]{2,1,0:T(1,128)S(1)}, f32[10,1,128]{2,1,0:T(1,128)S(1)}, u32[]{:S(2)}, u32[]{:S(2)}) collective-permute-start(f32[10,1,128]{2,1,0:T(1,128)S(1)} %get-tuple-element.51), channel_id=1, source_target_pairs={{1,0},{2,1},{3,2},{5,4},{6,5},{7,6},{9,8},{10,9},{11,10},{13,12},{... | collective-permute-start | bytes 15368 | tf_op jit(solution)/shard_map/ppermute | solution.py:25
  74.8 4.1 %collective-permute-done.7 = f32[10,1,128]{2,1,0:T(1,128)S(1)} collective-permute-done((f32[10,1,128]{2,1,0:T(1,128)S(1)}, f32[10,1,128]{2,1,0:T(1,128)S(1)}, u32[]{:S(2)}, u32[]{:S(2)}) %collective-permute-start.7) | collective-permute-done | bytes 5152 | tf_op jit(solution)/shard_map/ppermute | solution.py:24
  81.0 2.4 collective-permute-start.9
  83.5 3.4 collective-permute-done.9
  86.9 2.4 collective-permute-start.10
  90.7 4.1 %collective-permute-done.11 = f32[10,1,128]{2,1,0:T(1,128)S(1)} collective-permute-done((f32[10,1,128]{2,1,0:T(1,128)S(1)}, f32[10,1,128]{2,1,0:T(1,128)S(1)}, u32[]{:S(2)}, u32[]{:S(2)}) %collective-permute-start.11) | collective-permute-done | bytes 5152 | tf_op jit(solution)/shard_map/ppermute | solution.py:24
  94.9 5.5 %reshape.47 = f32[4,2,8,2,64,2]{5,4,3,2,1,0:T(8,128)} reshape(f32[8,16,128]{2,1,0:T(8,128)S(1)} %fusion.90) | data formatting | bytes 131072 | tf_op jit(solution)/shard_map/reshape | solution.py:102
  100.5 2.5 reduce_sum.144
  103.0 13.1 %all_gather.9 = f32[4,32,64]{2,0,1:T(4,128)S(1)} all-gather(f32[4,8,64]{2,0,1:T(4,128)S(1)} %copy.140), channel_id=1, replica_groups=mesh['wide'=8,'grp'=4] {'grp'}, dimensions={1}, use_global_device_ids=true | all-gather | bytes 40960 | tf_op jit(solution)/shard_map/all_gather | solution.py:46
  118.2 2.4 collective-permute-start.15
  120.7 3.5 collective-permute-done.15
  128.8 3.5 collective-permute-done.17
  136.7 2.4 collective-permute-start.21
  139.2 3.4 collective-permute-done.21
  143.3 12.4 %all-reduce.55 = (f32[]{:T(128)}, f32[]{:T(128)}) all-reduce(f32[]{:T(128)} %get-tuple-element.6, f32[]{:T(128)} %get-tuple-element.5), channel_id=1, replica_groups=mesh['wide'=8,'grp'=4] {'wide'}, use_global_device_ids=true, to_apply=%region_5.0 | all-reduce | flops 2 | bytes 16 | tf_op jit(solution)/shard_map/psum | solution.py:41
  157.6 12.4 %psum.86 = f32[]{:T(128)} all-reduce(f32[]{:T(128)} %multiply_reduce_fusion.8), channel_id=1, replica_groups=mesh['wide'=8,'grp'=4] {'wide'}, use_global_device_ids=true, to_apply=%region_11.0 | all-reduce | flops 1 | bytes 8 | tf_op jit(solution)/shard_map/psum | solution.py:41
  173.2 2.4 collective-permute-start.23
  175.7 3.4 collective-permute-done.23
  179.8 12.5 %psum.87 = f32[]{:T(128)} all-reduce(f32[]{:T(128)} %get-tuple-element.25), channel_id=1, replica_groups=mesh['wide'=8,'grp'=4] {'wide'}, use_global_device_ids=true, to_apply=%region_13.0 | all-reduce | flops 1 | bytes 8 | tf_op jit(solution)/shard_map/psum | solution.py:41
  194.2 12.4 %psum.88 = f32[]{:T(128)} all-reduce(f32[]{:T(128)} %get-tuple-element.23), channel_id=1, replica_groups=mesh['wide'=8,'grp'=4] {'wide'}, use_global_device_ids=true, to_apply=%region_15.0 | all-reduce | flops 1 | bytes 8 | tf_op jit(solution)/shard_map/psum | solution.py:41
  209.8 2.4 collective-permute-start.25
  212.3 3.4 collective-permute-done.25
  216.3 12.5 %psum.89 = f32[]{:T(128)} all-reduce(f32[]{:T(128)} %get-tuple-element.21), channel_id=1, replica_groups=mesh['wide'=8,'grp'=4] {'wide'}, use_global_device_ids=true, to_apply=%region_17.0 | all-reduce | flops 1 | bytes 8 | tf_op jit(solution)/shard_map/psum | solution.py:41
  230.7 12.4 %psum.90 = f32[]{:T(128)} all-reduce(f32[]{:T(128)} %get-tuple-element.19), channel_id=1, replica_groups=mesh['wide'=8,'grp'=4] {'wide'}, use_global_device_ids=true, to_apply=%region_19.0 | all-reduce | flops 1 | bytes 8 | tf_op jit(solution)/shard_map/psum | solution.py:41
  248.8 3.4 collective-permute-done.27
  252.9 12.5 %psum.91 = f32[]{:T(128)} all-reduce(f32[]{:T(128)} %get-tuple-element.17), channel_id=1, replica_groups=mesh['wide'=8,'grp'=4] {'wide'}, use_global_device_ids=true, to_apply=%region_21.0 | all-reduce | flops 1 | bytes 8 | tf_op jit(solution)/shard_map/psum | solution.py:41
  267.3 12.4 %psum.92 = f32[]{:T(128)} all-reduce(f32[]{:T(128)} %get-tuple-element.15), channel_id=1, replica_groups=mesh['wide'=8,'grp'=4] {'wide'}, use_global_device_ids=true, to_apply=%region_23.0 | all-reduce | flops 1 | bytes 8 | tf_op jit(solution)/shard_map/psum | solution.py:41
  285.4 3.4 collective-permute-done.29
  289.5 12.5 %psum.93 = f32[]{:T(128)} all-reduce(f32[]{:T(128)} %get-tuple-element.13), channel_id=1, replica_groups=mesh['wide'=8,'grp'=4] {'wide'}, use_global_device_ids=true, to_apply=%region_25.0 | all-reduce | flops 1 | bytes 8 | tf_op jit(solution)/shard_map/psum | solution.py:41
  303.8 12.4 %psum.94 = f32[]{:T(128)} all-reduce(f32[]{:T(128)} %multiply_reduce_fusion), channel_id=1, replica_groups=mesh['wide'=8,'grp'=4] {'wide'}, use_global_device_ids=true, to_apply=%region_27.0 | all-reduce | flops 1 | bytes 8 | tf_op jit(solution)/shard_map/psum | solution.py:41
  321.9 3.4 collective-permute-done.31
  326.0 12.5 %psum.95 = f32[]{:T(128)} all-reduce(f32[]{:T(128)} %fusion.123), channel_id=1, replica_groups=mesh['wide'=8,'grp'=4] {'wide'}, use_global_device_ids=true, to_apply=%region_29.0 | all-reduce | flops 1 | bytes 8 | tf_op jit(solution)/shard_map/psum | solution.py:41
  344.7 3.5 collective-permute-done.33
  352.7 3.5 collective-permute-done.35
  361.2 3.4 collective-permute-done.37
  367.4 4.1 %collective-permute-done.39 = f32[10,1,128]{2,1,0:T(1,128)S(1)} collective-permute-done((f32[10,1,128]{2,1,0:T(1,128)S(1)}, f32[10,1,128]{2,1,0:T(1,128)S(1)}, u32[]{:S(2)}, u32[]{:S(2)}) %collective-permute-start.39) | collective-permute-done | bytes 5152 | tf_op jit(solution)/shard_map/ppermute | solution.py:24
  376.0 3.4 collective-permute-done.41
  379.4 3.6 collective-permute-start.42
  384.5 4.1 %collective-permute-done.43 = f32[10,1,128]{2,1,0:T(1,128)S(1)} collective-permute-done((f32[10,1,128]{2,1,0:T(1,128)S(1)}, f32[10,1,128]{2,1,0:T(1,128)S(1)}, u32[]{:S(2)}, u32[]{:S(2)}) %collective-permute-start.43) | collective-permute-done | bytes 5152 | tf_op jit(solution)/shard_map/ppermute | solution.py:24
  (183 shorter events, 81.6 us)
Async XLA Ops:
  0.7 53.3 %collective-permute-start.1 = (f32[1,16,128]{2,1,0:T(8,128)S(1)}, f32[1,16,128]{2,1,0:T(8,128)S(1)}, u32[]{:S(2)}, u32[]{:S(2)}) collective-permute-start(f32[1,16,128]{2,1,0:T(8,128)S(1)} %get-tuple-element.94), channel_id=1, source_target_pairs={{0,4},{4,8},{8,12},{12,16},{16,20},{20,24},{24,28},{1,5},{5,9},{9,... | collective-permute-start | bytes 24584 | tf_op jit(solution)/shard_map/ppermute | solution.py:24
  2.6 51.4 %collective-permute-start = (f32[1,16,128]{2,1,0:T(8,128)S(1)}, f32[1,16,128]{2,1,0:T(8,128)S(1)}, u32[]{:S(2)}, u32[]{:S(2)}) collective-permute-start(f32[1,16,128]{2,1,0:T(8,128)S(1)} %get-tuple-element.95), channel_id=1, source_target_pairs={{4,0},{8,4},{12,8},{16,12},{20,16},{24,20},{28,24},{5,1},{9,5},{13... | collective-permute-start | bytes 24584 | tf_op jit(solution)/shard_map/ppermute | solution.py:25
  13.4 26.6 %copy-start = (f32[8,16,128]{2,1,0:T(8,128)S(1)}, f32[8,16,128]{2,1,0:T(8,128)}, u32[]{:S(2)}) copy-start(f32[8,16,128]{2,1,0:T(8,128)} %param.4) | copy-start | bytes 196612
  13.5 26.9 %copy-start.2 = (s32[8,16]{1,0:T(8,128)S(1)}, s32[8,16]{1,0:T(8,128)}, u32[]{:S(2)}) copy-start(s32[8,16]{1,0:T(8,128)} %param.5) | copy-start | bytes 1540
  13.5 48.1 %copy-start.1 = (f32[8,16,128]{2,1,0:T(8,128)S(1)}, f32[8,16,128]{2,1,0:T(8,128)}, u32[]{:S(2)}) copy-start(f32[8,16,128]{2,1,0:T(8,128)} %param.3) | copy-start | bytes 196612
  29.2 28.1 %collective-permute-start.13 = (f32[1,32,64]{2,1,0:T(8,128)S(1)}, f32[1,32,64]{2,1,0:T(8,128)S(1)}, u32[]{:S(2)}, u32[]{:S(2)}) collective-permute-start(f32[1,32,64]{2,1,0:T(8,128)S(1)} %get-tuple-element.83), channel_id=1, source_target_pairs={{0,4},{4,8},{8,12},{12,16},{16,20},{20,24},{24,28},{1,5},{5,9},{9,... | collective-permute-start | bytes 24584 | tf_op jit(solution)/shard_map/ppermute | solution.py:24
  33.6 18.2 %collective-permute-start.18 = (f32[1,16,32]{2,1,0:T(8,128)S(1)}, f32[1,16,32]{2,1,0:T(8,128)S(1)}, u32[]{:S(2)}, u32[]{:S(2)}) collective-permute-start(f32[1,16,32]{2,1,0:T(8,128)S(1)} %get-tuple-element.117), channel_id=1, source_target_pairs={{4,0},{8,4},{12,8},{16,12},{20,16},{24,20},{28,24},{5,1},{9,5},{13... | collective-permute-start | bytes 6152 | tf_op jit(solution)/shard_map/ppermute | solution.py:25
  38.1 15.9 %collective-permute-start.19 = (f32[1,16,32]{2,1,0:T(8,128)S(1)}, f32[1,16,32]{2,1,0:T(8,128)S(1)}, u32[]{:S(2)}, u32[]{:S(2)}) collective-permute-start(f32[1,16,32]{2,1,0:T(8,128)S(1)} %get-tuple-element.116), channel_id=1, source_target_pairs={{0,4},{4,8},{8,12},{12,16},{16,20},{20,24},{24,28},{1,5},{5,9},{9,... | collective-permute-start | bytes 6152 | tf_op jit(solution)/shard_map/ppermute | solution.py:24
  51.7 31.7 %collective-permute-start.12 = (f32[1,32,64]{2,1,0:T(8,128)S(1)}, f32[1,32,64]{2,1,0:T(8,128)S(1)}, u32[]{:S(2)}, u32[]{:S(2)}) collective-permute-start(f32[1,32,64]{2,1,0:T(8,128)S(1)} %get-tuple-element.82), channel_id=1, source_target_pairs={{4,0},{8,4},{12,8},{16,12},{20,16},{24,20},{28,24},{5,1},{9,5},{13... | collective-permute-start | bytes 24584 | tf_op jit(solution)/shard_map/ppermute | solution.py:25
  54.1 3.2 collective-permute-start.2
  56.0 5.6 %collective-permute-start.3 = (f32[10,1,128]{2,1,0:T(1,128)S(1)}, f32[10,1,128]{2,1,0:T(1,128)S(1)}, u32[]{:S(2)}, u32[]{:S(2)}) collective-permute-start(f32[10,1,128]{2,1,0:T(1,128)S(1)} %get-tuple-element.53), channel_id=1, source_target_pairs={{0,1},{1,2},{2,3},{4,5},{5,6},{6,7},{8,9},{9,10},{10,11},{12,13},{... | collective-permute-start | bytes 15368 | tf_op jit(solution)/shard_map/ppermute | solution.py:24
  61.7 4.4 %collective-permute-start.4 = (f32[1,16,128]{2,1,0:T(8,128)S(1)}, f32[1,16,128]{2,1,0:T(8,128)S(1)}, u32[]{:S(2)}, u32[]{:S(2)}) collective-permute-start(f32[1,16,128]{2,1,0:T(8,128)S(1)} %get-tuple-element.91), channel_id=1, source_target_pairs={{4,0},{8,4},{12,8},{16,12},{20,16},{24,20},{28,24},{5,1},{9,5},{13... | collective-permute-start | bytes 24584 | tf_op jit(solution)/shard_map/ppermute | solution.py:25
  63.6 5.9 %collective-permute-start.5 = (f32[1,16,128]{2,1,0:T(8,128)S(1)}, f32[1,16,128]{2,1,0:T(8,128)S(1)}, u32[]{:S(2)}, u32[]{:S(2)}) collective-permute-start(f32[1,16,128]{2,1,0:T(8,128)S(1)} %get-tuple-element.90), channel_id=1, source_target_pairs={{0,4},{4,8},{8,12},{12,16},{16,20},{20,24},{24,28},{1,5},{5,9},{9,... | collective-permute-start | bytes 24584 | tf_op jit(solution)/shard_map/ppermute | solution.py:24
  69.5 5.3 %collective-permute-start.6 = (f32[10,1,128]{2,1,0:T(1,128)S(1)}, f32[10,1,128]{2,1,0:T(1,128)S(1)}, u32[]{:S(2)}, u32[]{:S(2)}) collective-permute-start(f32[10,1,128]{2,1,0:T(1,128)S(1)} %get-tuple-element.51), channel_id=1, source_target_pairs={{1,0},{2,1},{3,2},{5,4},{6,5},{7,6},{9,8},{10,9},{11,10},{13,12},{... | collective-permute-start | bytes 15368 | tf_op jit(solution)/shard_map/ppermute | solution.py:25
  73.4 5.5 %collective-permute-start.7 = (f32[10,1,128]{2,1,0:T(1,128)S(1)}, f32[10,1,128]{2,1,0:T(1,128)S(1)}, u32[]{:S(2)}, u32[]{:S(2)}) collective-permute-start(f32[10,1,128]{2,1,0:T(1,128)S(1)} %get-tuple-element.52), channel_id=1, source_target_pairs={{0,1},{1,2},{2,3},{4,5},{5,6},{6,7},{8,9},{9,10},{10,11},{12,13},{... | collective-permute-start | bytes 15368 | tf_op jit(solution)/shard_map/ppermute | solution.py:24
  79.1 4.4 %collective-permute-start.8 = (f32[1,16,128]{2,1,0:T(8,128)S(1)}, f32[1,16,128]{2,1,0:T(8,128)S(1)}, u32[]{:S(2)}, u32[]{:S(2)}) collective-permute-start(f32[1,16,128]{2,1,0:T(8,128)S(1)} %get-tuple-element.87), channel_id=1, source_target_pairs={{4,0},{8,4},{12,8},{16,12},{20,16},{24,20},{28,24},{5,1},{9,5},{13... | collective-permute-start | bytes 24584 | tf_op jit(solution)/shard_map/ppermute | solution.py:25
  81.0 5.9 %collective-permute-start.9 = (f32[1,16,128]{2,1,0:T(8,128)S(1)}, f32[1,16,128]{2,1,0:T(8,128)S(1)}, u32[]{:S(2)}, u32[]{:S(2)}) collective-permute-start(f32[1,16,128]{2,1,0:T(8,128)S(1)} %get-tuple-element.86), channel_id=1, source_target_pairs={{0,4},{4,8},{8,12},{12,16},{16,20},{20,24},{24,28},{1,5},{5,9},{9,... | collective-permute-start | bytes 24584 | tf_op jit(solution)/shard_map/ppermute | solution.py:24
  86.9 3.8 collective-permute-start.10
  89.3 5.5 %collective-permute-start.11 = (f32[10,1,128]{2,1,0:T(1,128)S(1)}, f32[10,1,128]{2,1,0:T(1,128)S(1)}, u32[]{:S(2)}, u32[]{:S(2)}) collective-permute-start(f32[10,1,128]{2,1,0:T(1,128)S(1)} %get-tuple-element.50), channel_id=1, source_target_pairs={{0,1},{1,2},{2,3},{4,5},{5,6},{6,7},{8,9},{9,10},{10,11},{12,13},{... | collective-permute-start | bytes 15368 | tf_op jit(solution)/shard_map/ppermute | solution.py:24
  116.3 4.4 %collective-permute-start.14 = (f32[1,32,64]{2,1,0:T(8,128)S(1)}, f32[1,32,64]{2,1,0:T(8,128)S(1)}, u32[]{:S(2)}, u32[]{:S(2)}) collective-permute-start(f32[1,32,64]{2,1,0:T(8,128)S(1)} %get-tuple-element.79), channel_id=1, source_target_pairs={{4,0},{8,4},{12,8},{16,12},{20,16},{24,20},{28,24},{5,1},{9,5},{13... | collective-permute-start | bytes 24584 | tf_op jit(solution)/shard_map/ppermute | solution.py:25
  118.2 6.0 %collective-permute-start.15 = (f32[1,32,64]{2,1,0:T(8,128)S(1)}, f32[1,32,64]{2,1,0:T(8,128)S(1)}, u32[]{:S(2)}, u32[]{:S(2)}) collective-permute-start(f32[1,32,64]{2,1,0:T(8,128)S(1)} %get-tuple-element.78), channel_id=1, source_target_pairs={{0,4},{4,8},{8,12},{12,16},{16,20},{20,24},{24,28},{1,5},{5,9},{9,... | collective-permute-start | bytes 24584 | tf_op jit(solution)/shard_map/ppermute | solution.py:24
  124.3 4.4 %collective-permute-start.16 = (f32[1,32,64]{2,1,0:T(8,128)S(1)}, f32[1,32,64]{2,1,0:T(8,128)S(1)}, u32[]{:S(2)}, u32[]{:S(2)}) collective-permute-start(f32[1,32,64]{2,1,0:T(8,128)S(1)} %get-tuple-element.75), channel_id=1, source_target_pairs={{4,0},{8,4},{12,8},{16,12},{20,16},{24,20},{28,24},{5,1},{9,5},{13... | collective-permute-start | bytes 24584 | tf_op jit(solution)/shard_map/ppermute | solution.py:25
  126.3 6.0 %collective-permute-start.17 = (f32[1,32,64]{2,1,0:T(8,128)S(1)}, f32[1,32,64]{2,1,0:T(8,128)S(1)}, u32[]{:S(2)}, u32[]{:S(2)}) collective-permute-start(f32[1,32,64]{2,1,0:T(8,128)S(1)} %get-tuple-element.74), channel_id=1, source_target_pairs={{0,4},{4,8},{8,12},{12,16},{16,20},{20,24},{24,28},{1,5},{5,9},{9,... | collective-permute-start | bytes 24584 | tf_op jit(solution)/shard_map/ppermute | solution.py:24
  134.8 4.4 %collective-permute-start.20 = (f32[1,16,32]{2,1,0:T(8,128)S(1)}, f32[1,16,32]{2,1,0:T(8,128)S(1)}, u32[]{:S(2)}, u32[]{:S(2)}) collective-permute-start(f32[1,16,32]{2,1,0:T(8,128)S(1)} %get-tuple-element.121), channel_id=1, source_target_pairs={{4,0},{8,4},{12,8},{16,12},{20,16},{24,20},{28,24},{5,1},{9,5},{13... | collective-permute-start | bytes 6152 | tf_op jit(solution)/shard_map/ppermute | solution.py:25
  136.7 5.9 %collective-permute-start.21 = (f32[1,16,32]{2,1,0:T(8,128)S(1)}, f32[1,16,32]{2,1,0:T(8,128)S(1)}, u32[]{:S(2)}, u32[]{:S(2)}) collective-permute-start(f32[1,16,32]{2,1,0:T(8,128)S(1)} %get-tuple-element.120), channel_id=1, source_target_pairs={{0,4},{4,8},{8,12},{12,16},{16,20},{20,24},{24,28},{1,5},{5,9},{9,... | collective-permute-start | bytes 6152 | tf_op jit(solution)/shard_map/ppermute | solution.py:24
  171.3 4.4 %collective-permute-start.22 = (f32[1,16,32]{2,1,0:T(8,128)S(1)}, f32[1,16,32]{2,1,0:T(8,128)S(1)}, u32[]{:S(2)}, u32[]{:S(2)}) collective-permute-start(f32[1,16,32]{2,1,0:T(8,128)S(1)} %get-tuple-element.113), channel_id=1, source_target_pairs={{4,0},{8,4},{12,8},{16,12},{20,16},{24,20},{28,24},{5,1},{9,5},{13... | collective-permute-start | bytes 6152 | tf_op jit(solution)/shard_map/ppermute | solution.py:25
  173.2 5.9 %collective-permute-start.23 = (f32[1,16,32]{2,1,0:T(8,128)S(1)}, f32[1,16,32]{2,1,0:T(8,128)S(1)}, u32[]{:S(2)}, u32[]{:S(2)}) collective-permute-start(f32[1,16,32]{2,1,0:T(8,128)S(1)} %get-tuple-element.112), channel_id=1, source_target_pairs={{0,4},{4,8},{8,12},{12,16},{16,20},{20,24},{24,28},{1,5},{5,9},{9,... | collective-permute-start | bytes 6152 | tf_op jit(solution)/shard_map/ppermute | solution.py:24
  207.9 4.4 %collective-permute-start.24 = (f32[1,16,32]{2,1,0:T(8,128)S(1)}, f32[1,16,32]{2,1,0:T(8,128)S(1)}, u32[]{:S(2)}, u32[]{:S(2)}) collective-permute-start(f32[1,16,32]{2,1,0:T(8,128)S(1)} %get-tuple-element.109), channel_id=1, source_target_pairs={{4,0},{8,4},{12,8},{16,12},{20,16},{24,20},{28,24},{5,1},{9,5},{13... | collective-permute-start | bytes 6152 | tf_op jit(solution)/shard_map/ppermute | solution.py:25
  209.8 5.9 %collective-permute-start.25 = (f32[1,16,32]{2,1,0:T(8,128)S(1)}, f32[1,16,32]{2,1,0:T(8,128)S(1)}, u32[]{:S(2)}, u32[]{:S(2)}) collective-permute-start(f32[1,16,32]{2,1,0:T(8,128)S(1)} %get-tuple-element.108), channel_id=1, source_target_pairs={{0,4},{4,8},{8,12},{12,16},{16,20},{20,24},{24,28},{1,5},{5,9},{9,... | collective-permute-start | bytes 6152 | tf_op jit(solution)/shard_map/ppermute | solution.py:24
  244.4 4.4 %collective-permute-start.26 = (f32[1,16,32]{2,1,0:T(8,128)S(1)}, f32[1,16,32]{2,1,0:T(8,128)S(1)}, u32[]{:S(2)}, u32[]{:S(2)}) collective-permute-start(f32[1,16,32]{2,1,0:T(8,128)S(1)} %get-tuple-element.105), channel_id=1, source_target_pairs={{4,0},{8,4},{12,8},{16,12},{20,16},{24,20},{28,24},{5,1},{9,5},{13... | collective-permute-start | bytes 6152 | tf_op jit(solution)/shard_map/ppermute | solution.py:25
  246.3 5.9 %collective-permute-start.27 = (f32[1,16,32]{2,1,0:T(8,128)S(1)}, f32[1,16,32]{2,1,0:T(8,128)S(1)}, u32[]{:S(2)}, u32[]{:S(2)}) collective-permute-start(f32[1,16,32]{2,1,0:T(8,128)S(1)} %get-tuple-element.104), channel_id=1, source_target_pairs={{0,4},{4,8},{8,12},{12,16},{16,20},{20,24},{24,28},{1,5},{5,9},{9,... | collective-permute-start | bytes 6152 | tf_op jit(solution)/shard_map/ppermute | solution.py:24
  281.0 4.4 %collective-permute-start.28 = (f32[1,16,32]{2,1,0:T(8,128)S(1)}, f32[1,16,32]{2,1,0:T(8,128)S(1)}, u32[]{:S(2)}, u32[]{:S(2)}) collective-permute-start(f32[1,16,32]{2,1,0:T(8,128)S(1)} %get-tuple-element.101), channel_id=1, source_target_pairs={{4,0},{8,4},{12,8},{16,12},{20,16},{24,20},{28,24},{5,1},{9,5},{13... | collective-permute-start | bytes 6152 | tf_op jit(solution)/shard_map/ppermute | solution.py:25
  282.9 5.9 %collective-permute-start.29 = (f32[1,16,32]{2,1,0:T(8,128)S(1)}, f32[1,16,32]{2,1,0:T(8,128)S(1)}, u32[]{:S(2)}, u32[]{:S(2)}) collective-permute-start(f32[1,16,32]{2,1,0:T(8,128)S(1)} %get-tuple-element.100), channel_id=1, source_target_pairs={{0,4},{4,8},{8,12},{12,16},{16,20},{20,24},{24,28},{1,5},{5,9},{9,... | collective-permute-start | bytes 6152 | tf_op jit(solution)/shard_map/ppermute | solution.py:24
  317.5 4.4 %collective-permute-start.30 = (f32[1,16,32]{2,1,0:T(8,128)S(1)}, f32[1,16,32]{2,1,0:T(8,128)S(1)}, u32[]{:S(2)}, u32[]{:S(2)}) collective-permute-start(f32[1,16,32]{2,1,0:T(8,128)S(1)} %get-tuple-element.99), channel_id=1, source_target_pairs={{4,0},{8,4},{12,8},{16,12},{20,16},{24,20},{28,24},{5,1},{9,5},{13... | collective-permute-start | bytes 6152 | tf_op jit(solution)/shard_map/ppermute | solution.py:25
  319.4 5.9 %collective-permute-start.31 = (f32[1,16,32]{2,1,0:T(8,128)S(1)}, f32[1,16,32]{2,1,0:T(8,128)S(1)}, u32[]{:S(2)}, u32[]{:S(2)}) collective-permute-start(f32[1,16,32]{2,1,0:T(8,128)S(1)} %get-tuple-element.98), channel_id=1, source_target_pairs={{0,4},{4,8},{8,12},{12,16},{16,20},{20,24},{24,28},{1,5},{5,9},{9,... | collective-permute-start | bytes 6152 | tf_op jit(solution)/shard_map/ppermute | solution.py:24
  340.3 4.4 %collective-permute-start.32 = (f32[1,32,64]{2,1,0:T(8,128)S(1)}, f32[1,32,64]{2,1,0:T(8,128)S(1)}, u32[]{:S(2)}, u32[]{:S(2)}) collective-permute-start(f32[1,32,64]{2,1,0:T(8,128)S(1)} %get-tuple-element.69), channel_id=1, source_target_pairs={{4,0},{8,4},{12,8},{16,12},{20,16},{24,20},{28,24},{5,1},{9,5},{13... | collective-permute-start | bytes 24584 | tf_op jit(solution)/shard_map/ppermute | solution.py:25
  342.2 6.0 %collective-permute-start.33 = (f32[1,32,64]{2,1,0:T(8,128)S(1)}, f32[1,32,64]{2,1,0:T(8,128)S(1)}, u32[]{:S(2)}, u32[]{:S(2)}) collective-permute-start(f32[1,32,64]{2,1,0:T(8,128)S(1)} %get-tuple-element.68), channel_id=1, source_target_pairs={{0,4},{4,8},{8,12},{12,16},{16,20},{20,24},{24,28},{1,5},{5,9},{9,... | collective-permute-start | bytes 24584 | tf_op jit(solution)/shard_map/ppermute | solution.py:24
  348.3 4.4 %collective-permute-start.34 = (f32[1,32,64]{2,1,0:T(8,128)S(1)}, f32[1,32,64]{2,1,0:T(8,128)S(1)}, u32[]{:S(2)}, u32[]{:S(2)}) collective-permute-start(f32[1,32,64]{2,1,0:T(8,128)S(1)} %get-tuple-element.66), channel_id=1, source_target_pairs={{4,0},{8,4},{12,8},{16,12},{20,16},{24,20},{28,24},{5,1},{9,5},{13... | collective-permute-start | bytes 24584 | tf_op jit(solution)/shard_map/ppermute | solution.py:25
  350.2 6.0 %collective-permute-start.35 = (f32[1,32,64]{2,1,0:T(8,128)S(1)}, f32[1,32,64]{2,1,0:T(8,128)S(1)}, u32[]{:S(2)}, u32[]{:S(2)}) collective-permute-start(f32[1,32,64]{2,1,0:T(8,128)S(1)} %get-tuple-element.65), channel_id=1, source_target_pairs={{0,4},{4,8},{8,12},{12,16},{16,20},{20,24},{24,28},{1,5},{5,9},{9,... | collective-permute-start | bytes 24584 | tf_op jit(solution)/shard_map/ppermute | solution.py:24
  356.9 4.3 %collective-permute-start.36 = (f32[1,16,128]{2,1,0:T(8,128)S(1)}, f32[1,16,128]{2,1,0:T(8,128)S(1)}, u32[]{:S(2)}, u32[]{:S(2)}) collective-permute-start(f32[1,16,128]{2,1,0:T(8,128)S(1)} %get-tuple-element.60), channel_id=1, source_target_pairs={{4,0},{8,4},{12,8},{16,12},{20,16},{24,20},{28,24},{5,1},{9,5},{13... | collective-permute-start | bytes 24584 | tf_op jit(solution)/shard_map/ppermute | solution.py:25
  358.8 5.9 %collective-permute-start.37 = (f32[1,16,128]{2,1,0:T(8,128)S(1)}, f32[1,16,128]{2,1,0:T(8,128)S(1)}, u32[]{:S(2)}, u32[]{:S(2)}) collective-permute-start(f32[1,16,128]{2,1,0:T(8,128)S(1)} %get-tuple-element.59), channel_id=1, source_target_pairs={{0,4},{4,8},{8,12},{12,16},{16,20},{20,24},{24,28},{1,5},{5,9},{9,... | collective-permute-start | bytes 24584 | tf_op jit(solution)/shard_map/ppermute | solution.py:24
  364.7 2.7 collective-permute-start.38
  366.0 5.5 %collective-permute-start.39 = (f32[10,1,128]{2,1,0:T(1,128)S(1)}, f32[10,1,128]{2,1,0:T(1,128)S(1)}, u32[]{:S(2)}, u32[]{:S(2)}) collective-permute-start(f32[10,1,128]{2,1,0:T(1,128)S(1)} %get-tuple-element.48), channel_id=1, source_target_pairs={{0,1},{1,2},{2,3},{4,5},{5,6},{6,7},{8,9},{9,10},{10,11},{12,13},{... | collective-permute-start | bytes 15368 | tf_op jit(solution)/shard_map/ppermute | solution.py:24
  371.6 4.3 %collective-permute-start.40 = (f32[1,16,128]{2,1,0:T(8,128)S(1)}, f32[1,16,128]{2,1,0:T(8,128)S(1)}, u32[]{:S(2)}, u32[]{:S(2)}) collective-permute-start(f32[1,16,128]{2,1,0:T(8,128)S(1)} %get-tuple-element.58), channel_id=1, source_target_pairs={{4,0},{8,4},{12,8},{16,12},{20,16},{24,20},{28,24},{5,1},{9,5},{13... | collective-permute-start | bytes 24584 | tf_op jit(solution)/shard_map/ppermute | solution.py:25
  373.6 5.9 %collective-permute-start.41 = (f32[1,16,128]{2,1,0:T(8,128)S(1)}, f32[1,16,128]{2,1,0:T(8,128)S(1)}, u32[]{:S(2)}, u32[]{:S(2)}) collective-permute-start(f32[1,16,128]{2,1,0:T(8,128)S(1)} %get-tuple-element.57), channel_id=1, source_target_pairs={{0,4},{4,8},{8,12},{12,16},{16,20},{20,24},{24,28},{1,5},{5,9},{9,... | collective-permute-start | bytes 24584 | tf_op jit(solution)/shard_map/ppermute | solution.py:24
  379.4 5.0 %collective-permute-start.42 = (f32[10,1,128]{2,1,0:T(1,128)S(1)}, f32[10,1,128]{2,1,0:T(1,128)S(1)}, u32[]{:S(2)}, u32[]{:S(2)}) collective-permute-start(f32[10,1,128]{2,1,0:T(1,128)S(1)} %get-tuple-element.45), channel_id=1, source_target_pairs={{1,0},{2,1},{3,2},{5,4},{6,5},{7,6},{9,8},{10,9},{11,10},{13,12},{... | collective-permute-start | bytes 15368 | tf_op jit(solution)/shard_map/ppermute | solution.py:25
  383.1 5.5 %collective-permute-start.43 = (f32[10,1,128]{2,1,0:T(1,128)S(1)}, f32[10,1,128]{2,1,0:T(1,128)S(1)}, u32[]{:S(2)}, u32[]{:S(2)}) collective-permute-start(f32[10,1,128]{2,1,0:T(1,128)S(1)} %get-tuple-element.46), channel_id=1, source_target_pairs={{0,1},{1,2},{2,3},{4,5},{5,6},{6,7},{8,9},{9,10},{10,11},{12,13},{... | collective-permute-start | bytes 15368 | tf_op jit(solution)/shard_map/ppermute | solution.py:24
where the time goes:
time: 391 us; the launch traced here: 389 us
  blocking collectives  174 us (45%)
  starting transfers between devices  97.3 us (25%)
  waiting for transfers between devices  68.6 us (18%)
  local copies, waits for them, and re-layouts  19.4 us (5%)
  other arithmetic  15.3 us (4%)
  between operations  14.9 us (4%)
    psum x11, blocking collectives, sum_wide(): return lax.psum(partial_sum, 'wide')  137 us
    ppermute x22, waiting for transfers between devices, with_halo(): before = lax.ppermute(last, axis, up)  68.6 us
    ppermute x22, starting transfers between devices, with_halo(): after = lax.ppermute(initial, axis, down)  51.4 us
    ppermute x22, starting transfers between devices, with_halo(): before = lax.ppermute(last, axis, up)  45.9 us
    reshape x4, local copies, waits for them, and re-layouts, children_sum(): values.reshape(extent_x // 2, 2, extent_y // 2, 2, extent_z // 2, 2)  16.1 us
    all_gather x1, blocking collectives, agglomerate(): lax.all_gather(coef_field, 'grp', axis=1, tiled=True)  13.1 us
    all_gather x1, blocking collectives, agglomerate(): lax.all_gather(source_term, 'grp', axis=1, tiled=True)  13.1 us
    all_gather x1, blocking collectives, agglomerate(): lax.all_gather(heights, 'grp', axis=1, tiled=True)  10.6 us
  transfers between devices with their start and end apart: 44, of which 19 were waited for; matrix products, arithmetic and copies ran while one was open for 4% of the time, Pallas kernels for 0%

commit v1 on v0

v1 whole, which is shorter than its diff:
```python
import jax
import jax.numpy as jnp
from jax import lax
from jax.experimental import pallas as pl
from jax.experimental.pallas import tpu as pltpu
from jax.sharding import PartitionSpec as P

ITERS = 6
HALO = 8
TINY = 1e-30

cheb_center = (2.0 + 0.3) / 2.0
cheb_radius = (2.0 - 0.3) / 2.0
first_ratio = cheb_radius / cheb_center
second_ratio = 1.0 / (2.0 * cheb_center / cheb_radius - first_ratio)
carry_weight = second_ratio * first_ratio
fresh_weight = 2.0 * second_ratio / cheb_radius

DIRECTIONS = [(dx, dy) for dx in (-1, 0, 1) for dy in (-1, 0, 1) if (dx, dy) != (0, 0)]


def planes(low, high, body, carry=None):
    count = high - low
    unroll = count if count <= 32 else 4
    if carry is None:

        def step(x, _):
            body(x)
            return 0

        lax.fori_loop(low, high, step, 0, unroll=unroll)
        return None
    return lax.fori_loop(low, high, body, carry, unroll=unroll)


class Level:
    def __init__(self, count, width, depth, rep, wx, yp, ym, zp, zm, diag, inv, act):
        self.count, self.width, self.depth, self.rep = count, width, depth, rep
        self.wx, self.yp, self.ym, self.zp, self.zm = wx, yp, ym, zp, zm
        self.diag, self.inv, self.act = diag, inv, act

    def setup(self, coef, top):
        factor = float(self.rep)
        width, depth, rep = self.width, self.depth, self.rep
        lane = lax.broadcasted_iota(jnp.int32, (width, depth), 1)
        row = lax.broadcasted_iota(jnp.int32, (width, depth), 0)
        last_lane = lane >= depth - rep
        last_row = row == width - 1
        layer = ((lane // rep) * rep).astype(jnp.float32)

        def face(c, n):
            return factor * 2.0 * c * n / (c + n + TINY)

        self.wx[0] = jnp.zeros((width, depth), jnp.float32)

        def body(x):
            c = coef(x)
            plus_x = face(c, coef(x + 1))
            self.wx[x + 1] = plus_x
            plus_y = face(c, jnp.where(last_row, 0.0, pltpu.roll(c, width - 1, 0)))
            plus_z = face(c, jnp.where(last_lane, 0.0, pltpu.roll(c, depth - rep, 1)))
            minus_y = pltpu.roll(plus_y, 1, 0)
            minus_z = pltpu.roll(plus_z, rep, 1)
            above = jnp.where(last_lane, factor * c, plus_z)
            diag = plus_x + self.wx[x] + plus_y + minus_y + above + minus_z
            self.yp[x] = plus_y
            self.ym[x] = minus_y
            self.zp[x] = plus_z
            self.zm[x] = minus_z
            self.diag[x] = diag
            self.inv[x] = 1.0 / jnp.maximum(diag, TINY)
            self.act[x] = (layer < top(x)).astype(jnp.float32)

        planes(0, self.count, body)

    def apply(self, v, x):
        here = v[x + 1]
        coupled = self.wx[x + 1] * v[x + 2] + self.wx[x] * v[x]
        coupled = coupled + self.yp[x] * pltpu.roll(here, self.width - 1, 0)
        coupled = coupled + self.ym[x] * pltpu.roll(here, 1, 0)
        coupled = coupled + self.zp[x] * pltpu.roll(here, self.depth - self.rep, 1)
        coupled = coupled + self.zm[x] * pltpu.roll(here, self.rep, 1)
        return self.act[x] * (self.diag[x] * here - coupled)

    def smooth_fresh(self, f, u, out):
        def first(x):
            u[x + 1] = f[x] * self.inv[x] * (1.0 / cheb_center)

        planes(0, self.count, first)

        def second(x):
            residual = f[x] - self.apply(u, x)
            before = u[x + 1]
            update = carry_weight * before + fresh_weight * (residual * self.inv[x])
            out[x + 1] = before + update

        planes(0, self.count, second)

    def smooth_again(self, guess, f, e, u, low, high, put):
        def first(x):
            residual = f[x] - self.apply(guess, x)
            update = residual * self.inv[x] * (1.0 / cheb_center)
            e[x] = update
            u[x + 1] = guess[x + 1] + update

        planes(low - 1, high + 1, first)

        def second(x):
            residual = f[x] - self.apply(u, x)
            update = carry_weight * e[x] + fresh_weight * (residual * self.inv[x])
            put(x, u[x + 1] + update)

        planes(low, high, second)


def pair_lanes(values, rep, join):
    width, depth = values.shape
    lane = lax.broadcasted_iota(jnp.int32, (width, depth), 1)
    lower = (lane // rep) % 2 == 0
    partner = jnp.where(lower, pltpu.roll(values, depth - rep, 1), pltpu.roll(values, rep, 1))
    return join(values, partner)


def pair_rows(values, buffer, x, join):
    half = values.shape[0] // 2
    buffer[x] = values
    return join(buffer[x, pl.ds(0, half, stride=2)], buffer[x, pl.ds(1, half, stride=2)])


def keep_lane(values, slot, slots):
    width, depth = values.shape
    lane = lax.broadcasted_iota(jnp.int32, (width, depth), 1)
    kept = jnp.where(lane % slots == slot, values, 0.0)
    if slot:
        kept = pltpu.roll(kept, depth - slot, 1)
    shift = 1
    while shift < slots:
        kept = kept + pltpu.roll(kept, shift, 1)
        shift *= 2
    return kept


def add(a, b):
    return a + b


def kernel(wide, grp, source, conductivity, ice, out, *scratch):
    (fine, fw, f_load, f_u, f_smooth, f_e, pool_a, pool_b, pool_c,
     m_load, m_coef, m_top, mw, m_u, m_smooth, packed,
     outer, o_load, o_coef, o_top, ow, o_u, o_smooth, o_e, o_corr,
     pool_d, pool_e, pool_f, mine, gathered, g_coef, g_top, gw, g_x, g_r, g_d, g_a,
     spread, send_a, recv_a, send_b, recv_b, send_c, recv_c) = scratch
    bx, by, depth = source.shape
    bx1, by1, bx2, by2 = bx // 2, by // 2, bx // 4, by // 4
    x0, y0 = bx + 2 * HALO, by + 2 * HALO
    x1, y1 = x0 // 2, y0 // 2
    ring = bx1 + 1
    xo, yo = bx1 + 2 * ring, 3 * by1
    nx2, ny2 = wide * bx2, grp * by2
    w, g = lax.axis_index("wide"), lax.axis_index("grp")
    peers = wide * grp
    me = w * grp + g

    def clear(ref):
        def body(x):
            ref[x] = jnp.zeros(ref.shape[1:], ref.dtype)

        planes(0, ref.shape[0], body)

    for channel in range(3):
        clear(fine.at[channel])
    for channel in range(2):
        clear(outer.at[channel])

    barrier = pltpu.get_barrier_semaphore()

    def greet(d, _):
        other = lax.rem(me + d, peers)
        pl.semaphore_signal(barrier, inc=1, device_id=(other // grp, lax.rem(other, grp)),
                            device_id_type=pl.DeviceIdType.MESH)
        return 0

    lax.fori_loop(1, peers, greet, 0)

    rows16 = lax.broadcasted_iota(jnp.int32, (by, by), 0)
    cols16 = lax.broadcasted_iota(jnp.int32, (by, by), 1)
    eye = (rows16 == cols16).astype(jnp.float32)
    heights = ice[...].astype(jnp.float32)
    for x in range(bx):
        fine[0, HALO + x + 1, HALO:HALO + by] = source[x]
        fine[1, HALO + x + 1, HALO:HALO + by] = conductivity[x]
        column = jnp.sum(eye * heights[x:x + 1], axis=1, keepdims=True)
        fine[2, HALO + x + 1, HALO:HALO + by] = jnp.broadcast_to(column, (by, depth))
    for ref in (f_u, f_smooth, m_u, m_smooth, o_u, o_smooth, o_corr, g_d):
        ref[0] = jnp.zeros(ref.shape[1:], jnp.float32)
        ref[ref.shape[0] - 1] = jnp.zeros(ref.shape[1:], jnp.float32)
    for ref in (m_coef, o_coef, g_coef):
        ref[0] = jnp.zeros(ref.shape[1:], jnp.float32)
        ref[ref.shape[0] - 1] = jnp.zeros(ref.shape[1:], jnp.float32)
    clear_x = g_x.shape[0]
    for k in range(grp + 2):
        def blank(x):
            g_x[x, k] = jnp.zeros((by2, depth), jnp.float32)
        planes(0, clear_x, blank)

    pl.semaphore_wait(barrier, peers - 1)

    def inside(dx, dy):
        return (w + dx >= 0) & (w + dx < wide) & (g + dy >= 0) & (g + dy < grp)

    def copy_fine(k, dx, dy):
        src_x, dst_x, len_x = {
            1: (1 + bx, 1, HALO), 0: (1 + HALO, 1 + HALO, bx), -1: (1 + HALO, 1 + HALO + bx, HALO)
        }[dx]
        src_y, dst_y, len_y = {
            1: (by, 0, HALO), 0: (HALO, HALO, by), -1: (HALO, HALO + by, HALO)
        }[dy]
        return pltpu.make_async_remote_copy(
            src_ref=fine.at[:, pl.ds(src_x, len_x), pl.ds(src_y, len_y)],
            dst_ref=fine.at[:, pl.ds(dst_x, len_x), pl.ds(dst_y, len_y)],
            send_sem=send_a.at[k], recv_sem=recv_a.at[k],
            device_id=(w + dx, g + dy), device_id_type=pl.DeviceIdType.MESH)

    def copy_outer(k, dx, dy):
        src_x, dst_x, len_x = {
            1: (0, 0, ring), 0: (1, ring, bx1), -1: (1, ring + bx1, ring)
        }[dx]
        dst_y = {1: 0, 0: by1, -1: 2 * by1}[dy]
        return pltpu.make_async_remote_copy(
            src_ref=packed.at[:, pl.ds(src_x, len_x)],
            dst_ref=outer.at[:, pl.ds(dst_x, len_x), pl.ds(dst_y, by1)],
            send_sem=send_b.at[k], recv_sem=recv_b.at[k],
            device_id=(w + dx, g + dy), device_id_type=pl.DeviceIdType.MESH)

    def all_directions(make, sign, act):
        for k, (dx, dy) in enumerate(DIRECTIONS):
            @pl.when(inside(sign * dx, sign * dy))
            def _():
                act(make(k, dx, dy))

    all_directions(copy_fine, 1, lambda c: c.start())
    all_directions(copy_fine, -1, lambda c: c.wait_recv())

    level0 = Level(x0, y0, depth, 1, *fw)
    level0.setup(lambda x: fine[1, x + 1], lambda x: fine[2, x + 1])

    def load0(x):
        f_load[x] = level0.act[x] * fine[0, x + 1]

    planes(0, x0, load0)
    level0.smooth_fresh(f_load, f_u, f_smooth)

    def restrict0(x):
        a, b = 2 * x, 2 * x + 1
        rest = (f_load[a] - level0.apply(f_smooth, a)) + (f_load[b] - level0.apply(f_smooth, b))
        m_load[x] = pair_rows(pair_lanes(rest, 1, add), pool_a, x, add)
        coef = fine[1, a + 1] + fine[1, b + 1]
        m_coef[x + 1] = pair_rows(pair_lanes(coef, 1, add), pool_b, x, add) * 0.125
        top = jnp.maximum(fine[2, a + 1], fine[2, b + 1])
        m_top[x] = pair_rows(top, pool_c, x, jnp.maximum)

    planes(0, x1, restrict0)

    half = HALO // 2
    even = lax.broadcasted_iota(jnp.int32, (by1, depth), 1) % 2 == 0
    for r in range(bx1 + 2):
        x = half - 1 + r
        packed[0, r] = jnp.where(even, m_load[x, half:half + by1], m_coef[x + 1, half:half + by1])
        packed[1, r] = m_top[x, half:half + by1]
    all_directions(copy_outer, 1, lambda c: c.start())
    for r in range(bx1):
        for channel in range(2):
            outer[channel, ring + r, by1:2 * by1] = packed[channel, r + 1]

    level1 = Level(x1, y1, depth, 2, *mw)
    level1.setup(lambda x: m_coef[x + 1], lambda x: m_top[x])
    level1.smooth_fresh(m_load, m_u, m_smooth)
    quarter = half // 2
    slot = lax.broadcasted_iota(jnp.int32, (by2, depth), 1) % 4
    for x in range(bx2):
        a, b = half + 2 * x, half + 2 * x + 1
        rest = (m_load[a] - level1.apply(m_smooth, a)) + (m_load[b] - level1.apply(m_smooth, b))
        load = pair_rows(pair_lanes(rest, 2, add), pool_d, x, add)
        coef = pair_rows(pair_lanes(m_coef[a + 1] + m_coef[b + 1], 2, add), pool_e, x, add) * 0.125
        top = pair_rows(jnp.maximum(m_top[a], m_top[b]), pool_f, x, jnp.maximum)
        load, coef, top = (v[quarter:quarter + by2] for v in (load, coef, top))
        mine[x] = jnp.where(slot == 0, load, jnp.where(slot == 1, coef, top))

    def copy_coarse(d, from_w, from_g, to):
        return pltpu.make_async_remote_copy(
            src_ref=mine, dst_ref=gathered.at[from_g, pl.ds(from_w * bx2, bx2)],
            send_sem=send_c.at[d], recv_sem=recv_c.at[d],
            device_id=(to // grp, lax.rem(to, grp)), device_id_type=pl.DeviceIdType.MESH)

    def give(d, _):
        copy_coarse(d, w, g, lax.rem(me + d, peers)).start()
        return 0

    lax.fori_loop(1, peers, give, 0)
    for x in range(bx2):
        gathered[g, w * bx2 + x] = mine[x]

    all_directions(copy_outer, -1, lambda c: c.wait_recv())

    def unpack1(x):
        both = outer[0, x]
        o_load[x] = keep_lane(both, 0, 2)
        o_coef[x + 1] = keep_lane(both, 1, 2)

    planes(0, xo, unpack1)
    level_o = Level(xo, yo, depth, 2, *ow)
    level_o.setup(lambda x: o_coef[x + 1], lambda x: outer[1, x])
    level_o.smooth_fresh(o_load, o_u, o_smooth)

    def take(d, _):
        source_of = lax.rem(me + peers - d, peers)
        copy_coarse(d, source_of // grp, lax.rem(source_of, grp), me).wait_recv()
        return 0

    lax.fori_loop(1, peers, take, 0)

    def unpack2(x):
        for k in range(grp):
            g_a[x, k * by2:(k + 1) * by2] = gathered[k, x]
        everything = g_a[x]
        load = keep_lane(everything, 0, 4)
        g_r[x] = load
        g_d[x + 1] = load
        g_coef[x + 1] = keep_lane(everything, 1, 4)
        g_top[x] = keep_lane(everything, 2, 4)

    planes(0, nx2, unpack2)
    level2 = Level(nx2, ny2, depth, 4, *gw)
    level2.setup(lambda x: g_coef[x + 1], lambda x: g_top[x])
    zero = jnp.zeros((ny2, depth), jnp.float32)

    def total(values):
        return jnp.sum(values, axis=(0, 1), keepdims=True)

    current = total(planes(0, nx2, lambda x, acc: acc + g_r[x] * g_r[x], zero))
    sol = ow_sol = spread[1]

    def first_sol(x):
        sol[x] = zero

    planes(0, nx2, first_sol)

    def iterate(_, current):
        def image(x, acc):
            applied = level2.apply(g_d, x)
            g_a[x] = applied
            return acc + g_d[x + 1] * applied

        step = current / total(planes(0, nx2, image, zero))

        def move(x, acc):
            sol[x] = sol[x] + step * g_d[x + 1]
            residual = g_r[x] - step * g_a[x]
            g_r[x] = residual
            return acc + residual * residual

        following = total(planes(0, nx2, move, zero))
        ratio = following / current

        def turn(x):
            g_d[x + 1] = g_r[x] + ratio * g_d[x + 1]

        planes(0, nx2, turn)
        return following

    lax.fori_loop(0, ITERS, iterate, current)

    pad = 3

    def cut(x):
        for k in range(grp):
            g_x[x + pad, k + 1] = sol[x, k * by2:(k + 1) * by2]

    planes(0, nx2, cut)

    wide_rows = spread[0]
    for x in range(xo):
        parent = (x - ring) // 2
        for k in range(3):
            piece = g_x[w * bx2 + parent + pad, g + k]
            wide_rows[x, pl.ds(k * by1, by2, stride=2)] = piece
            wide_rows[x, pl.ds(k * by1 + 1, by2, stride=2)] = piece
        o_corr[x + 1] = o_smooth[x + 1] + level_o.act[x] * wide_rows[x]

    def put_outer(x, value):
        o_load[x] = value

    level_o.smooth_again(o_corr, o_load, o_e, o_u, ring - 1, ring + bx1 + 1, put_outer)

    fine_rows = spread[2]
    for x in range(HALO - 2, HALO + bx + 2):
        parent = o_load[(x - HALO) // 2 + ring, by1 - half:2 * by1 + half]
        fine_rows[x, pl.ds(0, y1, stride=2)] = parent
        fine_rows[x, pl.ds(1, y1, stride=2)] = parent
        f_smooth[x + 1] = f_smooth[x + 1] + level0.act[x] * fine_rows[x]

    def put_fine(x, value):
        out[x - HALO] = value[HALO:HALO + by]

    level0.smooth_again(f_smooth, f_load, f_e, f_u, HALO, HALO + bx, put_fine)

    all_directions(copy_fine, 1, lambda c: c.wait_send())
    all_directions(copy_outer, 1, lambda c: c.wait_send())

    def given(d, _):
        copy_coarse(d, w, g, lax.rem(me + d, peers)).wait_send()
        return 0

    lax.fori_loop(1, peers, given, 0)


def shards(source, conductivity, ice_cells):
    wide, grp = lax.axis_size("wide"), lax.axis_size("grp")
    bx, by, depth = source.shape
    bx1, by1, bx2, by2 = bx // 2, by // 2, bx // 4, by // 4
    x0, y0 = bx + 2 * HALO, by + 2 * HALO
    x1, y1 = x0 // 2, y0 // 2
    ring = bx1 + 1
    xo, yo = bx1 + 2 * ring, 3 * by1
    nx2, ny2 = wide * bx2, grp * by2
    peers = wide * grp

    def block(*shape):
        return pltpu.VMEM(shape + (depth,), jnp.float32)

    def held(count, width):
        return [block(count + 1, width)] + [block(count, width) for _ in range(7)]

    dma = pltpu.SemaphoreType.DMA
    scratch = [
        block(3, x0 + 2, y0), held(x0, y0), block(x0, y0), block(x0 + 2, y0), block(x0 + 2, y0),
        block(x0, y0), block(x1, y0), block(x1, y0), block(x1, y0),
        block(x1, y1), block(x1 + 2, y1), block(x1, y1), held(x1, y1), block(x1 + 2, y1),
        block(x1 + 2, y1), block(2, bx1 + 2, by1),
        block(2, xo, yo), block(xo, yo), block(xo + 2, yo), block(xo, yo), held(xo, yo),
        block(xo + 2, yo), block(xo + 2, yo), block(xo, yo), block(xo + 2, yo),
        block(bx2, y1), block(bx2, y1), block(bx2, y1), block(bx2, by2),
        block(grp, nx2, by2), block(nx2 + 2, ny2), block(nx2, ny2), held(nx2, ny2),
        block(nx2 + 6, grp + 2, by2), block(nx2, ny2), block(nx2 + 2, ny2), block(nx2, ny2),
        [block(xo, yo), block(nx2, ny2), block(x0, y0)],
        dma((8,)), dma((8,)), dma((8,)), dma((8,)), dma((peers,)), dma((peers,)),
    ]
    leaves, tree = jax.tree.flatten(scratch)

    def body(source_ref, conductivity_ref, ice_ref, out_ref, *refs):
        kernel(wide, grp, source_ref, conductivity_ref, ice_ref, out_ref,
               *jax.tree.unflatten(tree, refs))

    vmem = pl.BlockSpec(memory_space=pltpu.VMEM)
    return pl.pallas_call(
        body,
        out_shape=jax.ShapeDtypeStruct(source.shape, source.dtype),
        in_specs=[vmem] * 3,
        out_specs=vmem,
        scratch_shapes=leaves,
        compiler_params=pltpu.CompilerParams(
            collective_id=0, has_side_effects=True, vmem_limit_bytes=48 * 1024 * 1024
        ),
    )(source, conductivity, ice_cells)


def solution(mesh):
    placed = (P("wide", "grp", None), P("wide", "grp", None), P("wide", "grp"))
    return jax.shard_map(
        shards, mesh=mesh, in_specs=placed, out_specs=P("wide", "grp", None), check_vma=False
    )
```

time: 391 us -> 35.5 us (0.09)
  the two profiles are of different devices: /device:TPU:28 before, /device:TPU:0 now
where the time goes in v1:
time: 35.5 us; the launch traced here: 35.2 us
  Pallas kernels  32.2 us (91%)
  local copies, waits for them, and re-layouts  3 us (8%)
    pallas_call x1, Pallas kernels, shards(): pl.pallas_call(body, out_shape=jax.ShapeDtypeStruct(source.shape, source....  32.2 us
    unnamed x7, local copies, waits for them, and re-layouts  3 us

profile of v1, /device:TPU:0, one launch (start us, length us, event | category | flops | bytes accessed | tf_op | source)
XLA Modules:
  0.0 35.2 jit_solution(14414548691360792959)
XLA Ops:
  0.0 0.0 copy-start
  0.0 0.8 %copy-done = f32[8,16,128]{2,1,0:T(8,128)S(1)} copy-done((f32[8,16,128]{2,1,0:T(8,128)S(1)}, f32[8,16,128]{2,1,0:T(8,128)}, u32[]{:S(2)}) %copy-start) | copy-done | bytes 65560
  0.8 0.0 copy-start.1
  0.8 0.8 %copy-done.1 = f32[8,16,128]{2,1,0:T(8,128)S(1)} copy-done((f32[8,16,128]{2,1,0:T(8,128)S(1)}, f32[8,16,128]{2,1,0:T(8,128)}, u32[]{:S(2)}) %copy-start.1) | copy-done | bytes 65560
  1.7 0.0 copy-start.2
  1.7 0.7 %copy-done.2 = s32[8,16]{1,0:T(8,128)S(1)} copy-done((s32[8,16]{1,0:T(8,128)S(1)}, s32[8,16]{1,0:T(8,128)}, u32[]{:S(2)}) %copy-start.2) | copy-done | bytes 536
  2.4 32.2 %shard_map.37 = f32[8,16,128]{2,1,0:T(8,128)S(1)} custom-call(f32[8,16,128]{2,1,0:T(8,128)S(1)} %copy-done, f32[8,16,128]{2,1,0:T(8,128)S(1)} %copy-done.1, s32[8,16]{1,0:T(8,128)S(1)} %copy-done.2), custom_call_target="tpu_custom_call" | custom-call | tf_op jit(solution)/shard_map/pallas_call | solution.py:455
  34.6 0.6 %copy.5 = f32[8,16,128]{2,1,0:T(8,128)} copy(f32[8,16,128]{2,1,0:T(8,128)S(1)} %shard_map.37) | data formatting | bytes 131072
Async XLA Ops:
  0.0 0.8 %copy-start = (f32[8,16,128]{2,1,0:T(8,128)S(1)}, f32[8,16,128]{2,1,0:T(8,128)}, u32[]{:S(2)}) copy-start(f32[8,16,128]{2,1,0:T(8,128)} %source_ref.1) | copy-start | bytes 196612
  0.8 0.8 %copy-start.1 = (f32[8,16,128]{2,1,0:T(8,128)S(1)}, f32[8,16,128]{2,1,0:T(8,128)}, u32[]{:S(2)}) copy-start(f32[8,16,128]{2,1,0:T(8,128)} %conductivity_ref.1) | copy-start | bytes 196612
  1.7 0.7 %copy-start.2 = (s32[8,16]{1,0:T(8,128)S(1)}, s32[8,16]{1,0:T(8,128)}, u32[]{:S(2)}) copy-start(s32[8,16]{1,0:T(8,128)} %ice_ref.1) | copy-start | bytes 1540

commit v2 on v1

v2 whole, which is shorter than its diff:
```python
import jax
import jax.numpy as jnp
from jax import lax
from jax.experimental import pallas as pl
from jax.experimental.pallas import tpu as pltpu
from jax.sharding import PartitionSpec as P

ITERS = 6
HALO = 8
TINY = 1e-30

cheb_center = (2.0 + 0.3) / 2.0
cheb_radius = (2.0 - 0.3) / 2.0
first_ratio = cheb_radius / cheb_center
second_ratio = 1.0 / (2.0 * cheb_center / cheb_radius - first_ratio)
carry_weight = second_ratio * first_ratio
fresh_weight = 2.0 * second_ratio / cheb_radius

DIRECTIONS = [(dx, dy) for dx in (-1, 0, 1) for dy in (-1, 0, 1) if (dx, dy) != (0, 0)]


def planes(low, high, body, carry=None):
    count = high - low
    unroll = count if count <= 32 else 4
    if carry is None:

        def step(x, _):
            body(x)
            return 0

        lax.fori_loop(low, high, step, 0, unroll=unroll)
        return None
    return lax.fori_loop(low, high, body, carry, unroll=unroll)


class Level:
    def __init__(self, count, width, depth, rep, wx, yp, ym, zp, zm, diag, inv, act):
        self.count, self.width, self.depth, self.rep = count, width, depth, rep
        self.wx, self.yp, self.ym, self.zp, self.zm = wx, yp, ym, zp, zm
        self.diag, self.inv, self.act = diag, inv, act

    def setup(self, coef, top, low, high):
        factor = float(self.rep)
        width, depth, rep = self.width, self.depth, self.rep
        lane = lax.broadcasted_iota(jnp.int32, (width, depth), 1)
        row = lax.broadcasted_iota(jnp.int32, (width, depth), 0)
        last_lane = lane >= depth - rep
        last_row = row == width - 1
        layer = ((lane // rep) * rep).astype(jnp.float32)

        def face(c, n):
            return factor * 2.0 * c * n / (c + n + TINY)

        self.wx[low] = face(coef(low), coef(low - 1))

        def body(x):
            c = coef(x)
            plus_x = face(c, coef(x + 1))
            self.wx[x + 1] = plus_x
            plus_y = face(c, jnp.where(last_row, 0.0, pltpu.roll(c, width - 1, 0)))
            plus_z = face(c, jnp.where(last_lane, 0.0, pltpu.roll(c, depth - rep, 1)))
            minus_y = pltpu.roll(plus_y, 1, 0)
            minus_z = pltpu.roll(plus_z, rep, 1)
            above = jnp.where(last_lane, factor * c, plus_z)
            diag = plus_x + self.wx[x] + plus_y + minus_y + above + minus_z
            self.yp[x] = plus_y
            self.ym[x] = minus_y
            self.zp[x] = plus_z
            self.zm[x] = minus_z
            self.diag[x] = diag
            self.inv[x] = 1.0 / jnp.maximum(diag, TINY)
            self.act[x] = (layer < top(x)).astype(jnp.float32)

        planes(low, high, body)

    def apply(self, v, x):
        here = v[x + 1]
        coupled = self.wx[x + 1] * v[x + 2] + self.wx[x] * v[x]
        coupled = coupled + self.yp[x] * pltpu.roll(here, self.width - 1, 0)
        coupled = coupled + self.ym[x] * pltpu.roll(here, 1, 0)
        coupled = coupled + self.zp[x] * pltpu.roll(here, self.depth - self.rep, 1)
        coupled = coupled + self.zm[x] * pltpu.roll(here, self.rep, 1)
        return self.act[x] * (self.diag[x] * here - coupled)

    def smooth_fresh(self, f, u, out, low, high):
        def first(x):
            u[x + 1] = f[x] * self.inv[x] * (1.0 / cheb_center)

        planes(low, high, first)
        low, high = (low + 1, high - 1) if low else (low, high)

        def second(x):
            residual = f[x] - self.apply(u, x)
            before = u[x + 1]
            update = carry_weight * before + fresh_weight * (residual * self.inv[x])
            out[x + 1] = before + update

        planes(low, high, second)

    def smooth_again(self, guess, f, e, u, low, high, put):
        def first(x):
            residual = f[x] - self.apply(guess, x)
            update = residual * self.inv[x] * (1.0 / cheb_center)
            e[x] = update
            u[x + 1] = guess[x + 1] + update

        planes(low - 1, high + 1, first)

        def second(x):
            residual = f[x] - self.apply(u, x)
            update = carry_weight * e[x] + fresh_weight * (residual * self.inv[x])
            put(x, u[x + 1] + update)

        planes(low, high, second)


def pair_lanes(values, rep, join):
    width, depth = values.shape
    lane = lax.broadcasted_iota(jnp.int32, (width, depth), 1)
    lower = (lane // rep) % 2 == 0
    partner = jnp.where(lower, pltpu.roll(values, depth - rep, 1), pltpu.roll(values, rep, 1))
    return join(values, partner)


def pair_rows(values, buffer, x, join):
    half = values.shape[0] // 2
    buffer[x] = values
    return join(buffer[x, pl.ds(0, half, stride=2)], buffer[x, pl.ds(1, half, stride=2)])


def keep_lane(values, slot, slots):
    width, depth = values.shape
    lane = lax.broadcasted_iota(jnp.int32, (width, depth), 1)
    kept = jnp.where(lane % slots == slot, values, 0.0)
    if slot:
        kept = pltpu.roll(kept, depth - slot, 1)
    shift = 1
    while shift < slots:
        kept = kept + pltpu.roll(kept, shift, 1)
        shift *= 2
    return kept


def add(a, b):
    return a + b


def selector(count, first, stride, depth):
    rows = lax.broadcasted_iota(jnp.int32, (count, depth), 0)
    lanes = lax.broadcasted_iota(jnp.int32, (count, depth), 1)
    return (lanes == rows * stride + first).astype(jnp.float32)


def column(pick, row):
    return jnp.broadcast_to(jnp.sum(pick * row, axis=1, keepdims=True), pick.shape)


def kernel(wide, grp, source, conductivity, ice, out, *scratch):
    (fine, fw, f_load, f_u, f_smooth, f_e, f_top, pool_a, pool_b,
     m_load, m_coef, mw, m_u, m_smooth, packed,
     outer, o_load, o_coef, o_top, ow, o_u, o_smooth, o_e, o_corr,
     pool_d, pool_g, pool_h, mine, mine_c, gathered, gathered_c,
     g_coef, g_top, gw, g_x, g_r, g_d, g_a,
     spread, tops, ice_here, sem_in,
     send_a, recv_a, send_t, recv_t, send_s, recv_s, send_b, recv_b,
     send_c, recv_c, send_g, recv_g) = scratch
    bx, by, depth = source.shape
    bx1, by1, bx2, by2 = bx // 2, by // 2, bx // 4, by // 4
    x0, y0 = bx + 2 * HALO, by + 2 * HALO
    x1, y1 = x0 // 2, y0 // 2
    ring = bx1 + 1
    xo, yo = bx1 + 2 * ring, 3 * by1
    nx2, ny2 = wide * bx2, grp * by2
    half, quarter = HALO // 2, HALO // 4
    w, g = lax.axis_index("wide"), lax.axis_index("grp")
    peers = wide * grp
    me = w * grp + g

    middle = (pl.ds(HALO + 1, bx), pl.ds(HALO, by))
    load_source = pltpu.make_async_copy(source, fine.at[(0,) + middle], sem_in.at[0])
    load_coef = pltpu.make_async_copy(conductivity, fine.at[(1,) + middle], sem_in.at[1])
    load_ice = pltpu.make_async_copy(ice, ice_here, sem_in.at[2])
    load_ice.start()
    load_coef.start()
    load_source.start()

    for channel in range(2):
        for x in range(x0 + 2):
            if HALO < x <= HALO + bx:
                fine[channel, x, 0:HALO] = jnp.zeros((HALO, depth), jnp.float32)
                fine[channel, x, HALO + by:y0] = jnp.zeros((HALO, depth), jnp.float32)
            else:
                fine[channel, x] = jnp.zeros((y0, depth), jnp.float32)

    def clear(ref):
        def body(x):
            ref[x] = jnp.zeros(ref.shape[1:], ref.dtype)

        planes(0, ref.shape[0], body)

    clear(outer)
    clear(tops)

    barrier = pltpu.get_barrier_semaphore()

    def mesh_id(other):
        return (other // grp, lax.rem(other, grp))

    def greet(d, _):
        pl.semaphore_signal(barrier, inc=1, device_id=mesh_id(lax.rem(me + d, peers)),
                            device_id_type=pl.DeviceIdType.MESH)
        return 0

    lax.fori_loop(1, peers, greet, 0)

    for ref in (f_u, f_smooth, m_u, m_smooth, o_u, o_smooth, o_corr, g_d, m_coef, o_coef, g_coef):
        ref[0] = jnp.zeros(ref.shape[1:], jnp.float32)
        ref[ref.shape[0] - 1] = jnp.zeros(ref.shape[1:], jnp.float32)
    clear(g_x)

    load_ice.wait()
    tops[4, :, 0:by] = ice_here[...].astype(jnp.float32)
    load_coef.wait()
    slot = lax.broadcasted_iota(jnp.int32, (by2, depth), 1)
    sub = lax.broadcasted_iota(jnp.int32, (by2, depth), 0)
    chosen = slot % 4 == sub
    pick2 = selector(by2, 0, 4, depth)

    def fold(values):
        return jnp.sum(jnp.where(chosen, values, 0.0), axis=0, keepdims=True)

    all_tops = jnp.zeros((1, depth), jnp.float32)
    for x in range(bx2):
        coef = None
        for r in range(2):
            a = HALO + 1 + 4 * x + 2 * r
            pair = fine[1, a, HALO:HALO + by] + fine[1, a + 1, HALO:HALO + by]
            pair = pair_rows(pair_lanes(pair, 1, add), pool_g, 2 * x + r, add) * 0.125
            coef = pair if coef is None else coef + pair
        coef = pair_rows(pair_lanes(coef, 2, add), pool_h, x, add) * 0.125
        mine_c[x:x + 1] = fold(coef)
        top = jnp.max(tops[4, 4 * x:4 * x + 4], axis=0, keepdims=True)
        top = jnp.maximum(top, pltpu.roll(top, depth - 1, 1))
        top = jnp.maximum(top, pltpu.roll(top, depth - 2, 1))
        spot = slot // (depth // bx2) == x
        all_tops = all_tops + fold(jnp.where(spot, column(pick2, top), 0.0))
    mine_c[bx2:bx2 + 1] = all_tops

    load_source.wait()
    pl.semaphore_wait(barrier, peers - 1)

    def inside(dx, dy):
        return (w + dx >= 0) & (w + dx < wide) & (g + dy >= 0) & (g + dy < grp)

    def remote(src, dst, send, recv, device):
        return pltpu.make_async_remote_copy(
            src_ref=src, dst_ref=dst, send_sem=send, recv_sem=recv,
            device_id=device, device_id_type=pl.DeviceIdType.MESH)

    def copy_fine(channel, send, recv):
        def make(k, dx, dy):
            rows = HALO - 1 if dy == 0 else HALO - 2
            src_x, dst_x, len_x = {
                1: (1 + HALO + bx - rows, 1 + HALO - rows, rows),
                0: (1 + HALO, 1 + HALO, bx),
                -1: (1 + HALO, 1 + HALO + bx, rows),
            }[dx]
            src_y, dst_y, len_y = {
                1: (by, 0, HALO), 0: (HALO, HALO, by), -1: (HALO, HALO + by, HALO)
            }[dy]
            return remote(
                fine.at[channel, pl.ds(src_x, len_x), pl.ds(src_y, len_y)],
                fine.at[channel, pl.ds(dst_x, len_x), pl.ds(dst_y, len_y)],
                send.at[k], recv.at[k], (w + dx, g + dy))

        return make

    copy_coef = copy_fine(1, send_a, recv_a)
    copy_source = copy_fine(0, send_s, recv_s)

    def copy_tops(k, dx, dy):
        return remote(tops.at[4], tops.at[(1 - dx) * 3 + 1 - dy],
                      send_t.at[k], recv_t.at[k], (w + dx, g + dy))

    def copy_outer(k, dx, dy):
        src_x, dst_x, len_x = {
            1: (0, 0, ring), 0: (1, ring, bx1), -1: (1, ring + bx1, ring)
        }[dx]
        dst_y = {1: 0, 0: by1, -1: 2 * by1}[dy]
        return remote(packed.at[pl.ds(src_x, len_x)],
                      outer.at[pl.ds(dst_x, len_x), pl.ds(dst_y, by1)],
                      send_b.at[k], recv_b.at[k], (w + dx, g + dy))

    def all_directions(make, sign, act):
        for k, (dx, dy) in enumerate(DIRECTIONS):
            @pl.when(inside(sign * dx, sign * dy))
            def _():
                act(make(k, dx, dy))

    def copy_all(block, places, send, recv):
        def make(d, owner, to):
            return remote(block, places.at[owner], send.at[d], recv.at[d], mesh_id(to))

        def start():
            def body(d, _):
                make(d, me, lax.rem(me + d, peers)).start()
                return 0
            lax.fori_loop(1, peers, body, 0)

        def arrived():
            def body(d, _):
                make(d, lax.rem(me + peers - d, peers), me).wait_recv()
                return 0
            lax.fori_loop(1, peers, body, 0)

        def sent():
            def body(d, _):
                make(d, me, lax.rem(me + d, peers)).wait_send()
                return 0
            lax.fori_loop(1, peers, body, 0)

        return start, arrived, sent

    coarse_start, coarse_arrived, coarse_sent = copy_all(mine, gathered, send_c, recv_c)
    consts_start, consts_arrived, consts_sent = copy_all(mine_c, gathered_c, send_g, recv_g)

    all_directions(copy_coef, 1, lambda c: c.start())
    all_directions(copy_tops, 1, lambda c: c.start())
    all_directions(copy_source, 1, lambda c: c.start())
    consts_start()
    gathered_c[me] = mine_c[...]

    all_directions(copy_tops, -1, lambda c: c.wait_recv())
    reach = HALO - 2
    picks = (selector(HALO, by - HALO, 1, depth), selector(by, 0, 1, depth),
             selector(HALO, 0, 1, depth))
    starts = (0, HALO, HALO + by)
    for x in range(HALO - reach, HALO + bx + reach):
        row = x - HALO + bx
        for k in range(3):
            line = tops[row // bx * 3 + k, row % bx:row % bx + 1]
            f_top[x, starts[k]:starts[k] + picks[k].shape[0]] = column(picks[k], line)
    pick1 = selector(by1, 0, 2, depth)
    for x in range(1, xo - 1):
        row = 2 * (x - 1)
        for k in range(3):
            line = jnp.max(tops[row // bx * 3 + k, row % bx:row % bx + 2], axis=0, keepdims=True)
            line = jnp.maximum(line, pltpu.roll(line, depth - 1, 1))
            o_top[x, k * by1:(k + 1) * by1] = column(pick1, line)

    all_directions(copy_coef, -1, lambda c: c.wait_recv())
    level0 = Level(x0, y0, depth, 1, *fw)
    level0.setup(lambda x: fine[1, x + 1], lambda x: f_top[x], HALO - reach, HALO + bx + reach)

    def coef1(x):
        coef = fine[1, 2 * x + 1] + fine[1, 2 * x + 2]
        m_coef[x + 1] = pair_rows(pair_lanes(coef, 1, add), pool_b, x, add) * 0.125

    planes(half - 3, half + bx1 + 3, coef1)
    level1 = Level(x1, y1, depth, 2, *mw)
    level1.setup(lambda x: m_coef[x + 1], lambda x: o_top[x + ring - half, by1 - half:by1 - half + y1],
                 half - 2, half + bx1 + 2)

    all_directions(copy_source, -1, lambda c: c.wait_recv())

    def load0(x):
        f_load[x] = level0.act[x] * fine[0, x + 1]

    planes(HALO - reach, HALO + bx + reach, load0)
    level0.smooth_fresh(f_load, f_u, f_smooth, HALO - reach, HALO + bx + reach)

    def restrict0(x):
        a, b = 2 * x, 2 * x + 1
        rest = (f_load[a] - level0.apply(f_smooth, a)) + (f_load[b] - level0.apply(f_smooth, b))
        m_load[x] = pair_rows(pair_lanes(rest, 1, add), pool_a, x, add)

    planes(half - 2, half + bx1 + 2, restrict0)

    even = lax.broadcasted_iota(jnp.int32, (by1, depth), 1) % 2 == 0
    for r in range(bx1 + 2):
        x = half - 1 + r
        packed[r] = jnp.where(even, m_load[x, half:half + by1], m_coef[x + 1, half:half + by1])
    all_directions(copy_outer, 1, lambda c: c.start())
    for r in range(bx1):
        outer[ring + r, by1:2 * by1] = packed[r + 1]

    level1.smooth_fresh(m_load, m_u, m_smooth, half - 2, half + bx1 + 2)
    for x in range(bx2):
        a, b = half + 2 * x, half + 2 * x + 1
        rest = (m_load[a] - level1.apply(m_smooth, a)) + (m_load[b] - level1.apply(m_smooth, b))
        load = pair_rows(pair_lanes(rest, 2, add), pool_d, x, add)
        mine[x:x + 1] = fold(load[quarter:quarter + by2])

    coarse_start()
    gathered[me] = mine[...]

    consts_arrived()
    lanes2 = lax.broadcasted_iota(jnp.int32, (ny2, depth), 1)
    chosen2 = lanes2 % 4 == lax.broadcasted_iota(jnp.int32, (ny2, depth), 0) % 4

    def unfold(places, x, row):
        for k in range(grp):
            line = places[(x // bx2) * grp + k, pl.ds(row, 1)]
            g_a[x, k * by2:(k + 1) * by2] = jnp.broadcast_to(line, (by2, depth))
        return jnp.where(chosen2, g_a[x], 0.0)

    def widen(values):
        return pair_lanes(pair_lanes(values, 1, add), 2, add)

    def unpack_consts(x):
        g_coef[x + 1] = widen(unfold(gathered_c, x, x % bx2))
        part = unfold(gathered_c, x, bx2)
        spot = lanes2 // (depth // bx2) == x % bx2
        top = jnp.max(jnp.where(spot, part, 0.0), axis=1, keepdims=True)
        g_top[x] = jnp.broadcast_to(top, (ny2, depth))

    planes(0, nx2, unpack_consts)
    level2 = Level(nx2, ny2, depth, 4, *gw)
    level2.setup(lambda x: g_coef[x + 1], lambda x: g_top[x], 0, nx2)

    all_directions(copy_outer, -1, lambda c: c.wait_recv())

    def unpack1(x):
        both = outer[x]
        o_load[x] = keep_lane(both, 0, 2)
        o_coef[x + 1] = keep_lane(both, 1, 2)

    planes(0, xo, unpack1)
    level_o = Level(xo, yo, depth, 2, *ow)
    level_o.setup(lambda x: o_coef[x + 1], lambda x: o_top[x], 1, xo - 1)
    level_o.smooth_fresh(o_load, o_u, o_smooth, 1, xo - 1)

    coarse_arrived()

    def unpack2(x):
        load = widen(unfold(gathered, x, x % bx2))
        g_r[x] = load
        g_d[x + 1] = load

    planes(0, nx2, unpack2)
    zero = jnp.zeros((ny2, depth), jnp.float32)

    def total(values):
        return jnp.sum(values, axis=(0, 1), keepdims=True)

    current = total(planes(0, nx2, lambda x, acc: acc + g_r[x] * g_r[x], zero))
    sol = spread[1]

    def first_sol(x):
        sol[x] = zero

    planes(0, nx2, first_sol)

    def iterate(_, current):
        def image(x, acc):
            applied = level2.apply(g_d, x)
            g_a[x] = applied
            return acc + g_d[x + 1] * applied

        step = current / total(planes(0, nx2, image, zero))

        def move(x, acc):
            sol[x] = sol[x] + step * g_d[x + 1]
            residual = g_r[x] - step * g_a[x]
            g_r[x] = residual
            return acc + residual * residual

        following = total(planes(0, nx2, move, zero))
        ratio = following / current

        def turn(x):
            g_d[x + 1] = g_r[x] + ratio * g_d[x + 1]

        planes(0, nx2, turn)
        return following

    lax.fori_loop(0, ITERS, iterate, current)

    pad = 3

    def cut(x):
        for k in range(grp):
            g_x[x + pad, k + 1] = sol[x, k * by2:(k + 1) * by2]

    planes(0, nx2, cut)

    wide_rows = spread[0]
    for x in range(2, xo - 2):
        parent = (x - ring) // 2
        for k in range(3):
            piece = g_x[w * bx2 + parent + pad, g + k]
            wide_rows[x, pl.ds(k * by1, by2, stride=2)] = piece
            wide_rows[x, pl.ds(k * by1 + 1, by2, stride=2)] = piece
        o_corr[x + 1] = o_smooth[x + 1] + level_o.act[x] * wide_rows[x]

    def put_outer(x, value):
        o_load[x] = value

    level_o.smooth_again(o_corr, o_load, o_e, o_u, ring - 1, ring + bx1 + 1, put_outer)

    fine_rows = spread[2]
    for x in range(HALO - 2, HALO + bx + 2):
        parent = o_load[(x - HALO) // 2 + ring, by1 - half:2 * by1 + half]
        fine_rows[x, pl.ds(0, y1, stride=2)] = parent
        fine_rows[x, pl.ds(1, y1, stride=2)] = parent
        f_smooth[x + 1] = f_smooth[x + 1] + level0.act[x] * fine_rows[x]

    def put_fine(x, value):
        out[x - HALO] = value[HALO:HALO + by]

    level0.smooth_again(f_smooth, f_load, f_e, f_u, HALO, HALO + bx, put_fine)

    for make in (copy_coef, copy_tops, copy_source, copy_outer):
        all_directions(make, 1, lambda c: c.wait_send())
    consts_sent()
    coarse_sent()


def shards(source, conductivity, ice_cells):
    wide, grp = lax.axis_size("wide"), lax.axis_size("grp")
    bx, by, depth = source.shape
    bx1, by1, bx2, by2 = bx // 2, by // 2, bx // 4, by // 4
    x0, y0 = bx + 2 * HALO, by + 2 * HALO
    x1, y1 = x0 // 2, y0 // 2
    ring = bx1 + 1
    xo, yo = bx1 + 2 * ring, 3 * by1
    nx2, ny2 = wide * bx2, grp * by2
    peers = wide * grp

    def block(*shape):
        return pltpu.VMEM(shape + (depth,), jnp.float32)

    def held(count, width):
        return [block(count + 1, width)] + [block(count, width) for _ in range(7)]

    dma = pltpu.SemaphoreType.DMA
    scratch = [
        block(2, x0 + 2, y0), held(x0, y0), block(x0, y0), block(x0 + 2, y0), block(x0 + 2, y0),
        block(x0, y0), block(x0, y0), block(x1, y0), block(x1, y0),
        block(x1, y1), block(x1 + 2, y1), held(x1, y1), block(x1 + 2, y1),
        block(x1 + 2, y1), block(bx1 + 2, by1),
        block(xo, yo), block(xo, yo), block(xo + 2, yo), block(xo, yo), held(xo, yo),
        block(xo + 2, yo), block(xo + 2, yo), block(xo, yo), block(xo + 2, yo),
        block(bx2, y1), block(bx1, by), block(bx2, by1), block(bx2), block(bx2 + 1),
        block(peers, bx2), block(peers, bx2 + 1),
        block(nx2 + 2, ny2), block(nx2, ny2), held(nx2, ny2),
        block(nx2 + 6, grp + 2, by2), block(nx2, ny2), block(nx2 + 2, ny2), block(nx2, ny2),
        [block(xo, yo), block(nx2, ny2), block(x0, y0)],
        block(9, bx), pltpu.VMEM((bx, by), jnp.int32), dma((3,)),
        *[dma((8,)) for _ in range(8)], *[dma((peers,)) for _ in range(4)],
    ]
    leaves, tree = jax.tree.flatten(scratch)

    def body(source_ref, conductivity_ref, ice_ref, out_ref, *refs):
        kernel(wide, grp, source_ref, conductivity_ref, ice_ref, out_ref,
               *jax.tree.unflatten(tree, refs))

    vmem = pl.BlockSpec(memory_space=pltpu.VMEM)
    return pl.pallas_call(
        body,
        out_shape=jax.ShapeDtypeStruct(source.shape, source.dtype),
        in_specs=[pl.BlockSpec(memory_space=pltpu.HBM)] * 3,
        out_specs=vmem,
        scratch_shapes=leaves,
        compiler_params=pltpu.CompilerParams(
            collective_id=0, has_side_effects=True, vmem_limit_bytes=48 * 1024 * 1024
        ),
    )(source, conductivity, ice_cells)


def solution(mesh):
    placed = (P("wide", "grp", None), P("wide", "grp", None), P("wide", "grp"))
    return jax.shard_map(
        shards, mesh=mesh, in_specs=placed, out_specs=P("wide", "grp", None), check_vma=False
    )
```

time: 35.5 us -> 28.4 us (0.80)
  Pallas kernels: 32.2 us -> 25.2 us
    pallas_call x1, Pallas kernels: 32.2 us -> 25.2 us  [shards(): pl.pallas_call(body, out_shape=jax.ShapeDtypeStruct(source.shape, source....]
where the time goes in v2:
time: 28.4 us; the launch traced here: 28.2 us
  Pallas kernels  25.2 us (89%)
  local copies, waits for them, and re-layouts  3 us (11%)
    pallas_call x1, Pallas kernels, shards(): pl.pallas_call(body, out_shape=jax.ShapeDtypeStruct(source.shape, source....  25.2 us
    unnamed x7, local copies, waits for them, and re-layouts  3 us

profile of v2, /device:TPU:0, one launch (start us, length us, event | category | flops | bytes accessed | tf_op | source)
XLA Modules:
  0.0 28.2 jit_solution(11147155940295809687)
XLA Ops:
  0.0 0.0 copy-start
  0.0 0.8 %copy-done = f32[8,16,128]{2,1,0:T(8,128)S(1)} copy-done((f32[8,16,128]{2,1,0:T(8,128)S(1)}, f32[8,16,128]{2,1,0:T(8,128)}, u32[]{:S(2)}) %copy-start) | copy-done | bytes 65560
  0.8 0.0 copy-start.1
  0.8 0.8 %copy-done.1 = f32[8,16,128]{2,1,0:T(8,128)S(1)} copy-done((f32[8,16,128]{2,1,0:T(8,128)S(1)}, f32[8,16,128]{2,1,0:T(8,128)}, u32[]{:S(2)}) %copy-start.1) | copy-done | bytes 65560
  1.7 0.0 copy-start.2
  1.7 0.7 %copy-done.2 = s32[8,16]{1,0:T(8,128)S(1)} copy-done((s32[8,16]{1,0:T(8,128)S(1)}, s32[8,16]{1,0:T(8,128)}, u32[]{:S(2)}) %copy-start.2) | copy-done | bytes 536
  2.4 25.2 %shard_map.37 = f32[8,16,128]{2,1,0:T(8,128)S(1)} custom-call(f32[8,16,128]{2,1,0:T(8,128)S(1)} %copy-done, f32[8,16,128]{2,1,0:T(8,128)S(1)} %copy-done.1, s32[8,16]{1,0:T(8,128)S(1)} %copy-done.2), custom_call_target="tpu_custom_call" | custom-call | tf_op jit(solution)/shard_map/pallas_call | solution.py:559
  27.6 0.6 %copy.5 = f32[8,16,128]{2,1,0:T(8,128)} copy(f32[8,16,128]{2,1,0:T(8,128)S(1)} %shard_map.37) | data formatting | bytes 131072
Async XLA Ops:
  0.0 0.8 %copy-start = (f32[8,16,128]{2,1,0:T(8,128)S(1)}, f32[8,16,128]{2,1,0:T(8,128)}, u32[]{:S(2)}) copy-start(f32[8,16,128]{2,1,0:T(8,128)} %source_ref.1) | copy-start | bytes 196612
  0.8 0.8 %copy-start.1 = (f32[8,16,128]{2,1,0:T(8,128)S(1)}, f32[8,16,128]{2,1,0:T(8,128)}, u32[]{:S(2)}) copy-start(f32[8,16,128]{2,1,0:T(8,128)} %conductivity_ref.1) | copy-start | bytes 196612
  1.7 0.7 %copy-start.2 = (s32[8,16]{1,0:T(8,128)S(1)}, s32[8,16]{1,0:T(8,128)}, u32[]{:S(2)}) copy-start(s32[8,16]{1,0:T(8,128)} %ice_ref.1) | copy-start | bytes 1540

commit v3 on v2

--- a/solution.py
+++ b/solution.py
@@ -114,6 +114,55 @@
         planes(low, high, second)
 
 
+class Coarse:
+    def __init__(self, count, width, depth, px, mx, yp, ym, zp, zm, diag, act):
+        self.count, self.width, self.depth = count, width, depth
+        self.px, self.mx, self.yp, self.ym, self.zp, self.zm = px, mx, yp, ym, zp, zm
+        self.diag, self.act = diag, act
+        self.lane = lax.broadcasted_iota(jnp.int32, (width, depth), 1)
+        self.slot = self.lane % 4
+
+    def beside_x(self, v, x):
+        here, depth = v[x + 1], self.depth
+        after = jnp.where(self.slot < 3, pltpu.roll(here, depth - 1, 1), pltpu.roll(v[x + 2], 3, 1))
+        before = jnp.where(self.slot > 0, pltpu.roll(here, 1, 1), pltpu.roll(v[x], depth - 3, 1))
+        return here, after, before
+
+    def setup(self, coef, top):
+        width, depth = self.width, self.depth
+        last_row = lax.broadcasted_iota(jnp.int32, (width, depth), 0) == width - 1
+        last_lane = self.lane >= depth - 4
+        layer = (self.lane - self.slot).astype(jnp.float32)
+
+        def face(c, n):
+            return 8.0 * c * n / (c + n + TINY)
+
+        def body(x):
+            c, after, before = self.beside_x(coef, x)
+            plus_x, minus_x = face(c, after), face(c, before)
+            plus_y = face(c, jnp.where(last_row, 0.0, pltpu.roll(c, width - 1, 0)))
+            plus_z = face(c, jnp.where(last_lane, 0.0, pltpu.roll(c, depth - 4, 1)))
+            minus_y = pltpu.roll(plus_y, 1, 0)
+            minus_z = pltpu.roll(plus_z, 4, 1)
+            above = jnp.where(last_lane, 4.0 * c, plus_z)
+            self.diag[x] = plus_x + minus_x + plus_y + minus_y + above + minus_z
+            self.px[x], self.mx[x] = plus_x, minus_x
+            self.yp[x], self.ym[x] = plus_y, minus_y
+            self.zp[x], self.zm[x] = plus_z, minus_z
+            self.act[x] = (layer < top[x]).astype(jnp.float32)
+
+        planes(0, self.count, body)
+
+    def apply(self, v, x):
+        here, after, before = self.beside_x(v, x)
+        coupled = self.px[x] * after + self.mx[x] * before
+        coupled = coupled + self.yp[x] * pltpu.roll(here, self.width - 1, 0)
+        coupled = coupled + self.ym[x] * pltpu.roll(here, 1, 0)
+        coupled = coupled + self.zp[x] * pltpu.roll(here, self.depth - 4, 1)
+        coupled = coupled + self.zm[x] * pltpu.roll(here, 4, 1)
+        return here, self.act[x] * (self.diag[x] * here - coupled)
+
+
 def pair_lanes(values, rep, join):
     width, depth = values.shape
     lane = lax.broadcasted_iota(jnp.int32, (width, depth), 1)
@@ -160,8 +209,8 @@
      m_load, m_coef, mw, m_u, m_smooth, packed,
      outer, o_load, o_coef, o_top, ow, o_u, o_smooth, o_e, o_corr,
      pool_d, pool_g, pool_h, mine, mine_c, gathered, gathered_c,
-     g_coef, g_top, gw, g_x, g_r, g_d, g_a,
-     spread, tops, ice_here, sem_in,
+     g_coef, g_top, gw, g_x, g_r, g_p, g_s, g_a, sol,
+     wide_rows, fine_rows, tops, ice_here, sem_in,
      send_a, recv_a, send_t, recv_t, send_s, recv_s, send_b, recv_b,
      send_c, recv_c, send_g, recv_g) = scratch
     bx, by, depth = source.shape
@@ -213,7 +262,7 @@
 
     lax.fori_loop(1, peers, greet, 0)
 
-    for ref in (f_u, f_smooth, m_u, m_smooth, o_u, o_smooth, o_corr, g_d, m_coef, o_coef, g_coef):
+    for ref in (f_u, f_smooth, m_u, m_smooth, o_u, o_smooth, o_corr, g_r, sol, m_coef, o_coef, g_coef):
         ref[0] = jnp.zeros(ref.shape[1:], jnp.float32)
         ref[ref.shape[0] - 1] = jnp.zeros(ref.shape[1:], jnp.float32)
     clear(g_x)
@@ -221,15 +270,10 @@
     load_ice.wait()
     tops[4, :, 0:by] = ice_here[...].astype(jnp.float32)
     load_coef.wait()
-    slot = lax.broadcasted_iota(jnp.int32, (by2, depth), 1)
-    sub = lax.broadcasted_iota(jnp.int32, (by2, depth), 0)
-    chosen = slot % 4 == sub
+    slot = lax.broadcasted_iota(jnp.int32, (by2, depth), 1) % 4
     pick2 = selector(by2, 0, 4, depth)
-
-    def fold(values):
-        return jnp.sum(jnp.where(chosen, values, 0.0), axis=0, keepdims=True)
-
-    all_tops = jnp.zeros((1, depth), jnp.float32)
+    first_slot = lax.rem(w * bx2, 4)
+    consts = jnp.zeros((by2, depth), jnp.float32)
     for x in range(bx2):
         coef = None
         for r in range(2):
@@ -238,13 +282,13 @@
             pair = pair_rows(pair_lanes(pair, 1, add), pool_g, 2 * x + r, add) * 0.125
             coef = pair if coef is None else coef + pair
         coef = pair_rows(pair_lanes(coef, 2, add), pool_h, x, add) * 0.125
-        mine_c[x:x + 1] = fold(coef)
         top = jnp.max(tops[4, 4 * x:4 * x + 4], axis=0, keepdims=True)
         top = jnp.maximum(top, pltpu.roll(top, depth - 1, 1))
         top = jnp.maximum(top, pltpu.roll(top, depth - 2, 1))
-        spot = slot // (depth // bx2) == x
-        all_tops = all_tops + fold(jnp.where(spot, column(pick2, top), 0.0))
-    mine_c[bx2:bx2 + 1] = all_tops
+        here = first_slot + x
+        consts = jnp.where(slot == here, coef, consts)
+        consts = jnp.where(slot == lax.rem(here + 2, 4), column(pick2, top), consts)
+    mine_c[...] = consts
 
     load_source.wait()
     pl.semaphore_wait(barrier, peers - 1)
@@ -259,7 +303,7 @@
 
     def copy_fine(channel, send, recv):
         def make(k, dx, dy):
-            rows = HALO - 1 if dy == 0 else HALO - 2
+            rows = (HALO - 2 if dy == 0 else HALO - 3) + channel
             src_x, dst_x, len_x = {
                 1: (1 + HALO + bx - rows, 1 + HALO - rows, rows),
                 0: (1 + HALO, 1 + HALO, bx),
@@ -385,38 +429,46 @@
         outer[ring + r, by1:2 * by1] = packed[r + 1]
 
     level1.smooth_fresh(m_load, m_u, m_smooth, half - 2, half + bx1 + 2)
+    rows = by2 // 2
+    loads = jnp.zeros((rows, depth), jnp.float32)
     for x in range(bx2):
         a, b = half + 2 * x, half + 2 * x + 1
         rest = (m_load[a] - level1.apply(m_smooth, a)) + (m_load[b] - level1.apply(m_smooth, b))
         load = pair_rows(pair_lanes(rest, 2, add), pool_d, x, add)
-        mine[x:x + 1] = fold(load[quarter:quarter + by2])
+        here = first_slot + x
+        loads = jnp.where(slot[:rows] == here, load[quarter:quarter + rows], loads)
+        loads = jnp.where(slot[:rows] == lax.rem(here + 2, 4),
+                          load[quarter + rows:quarter + by2], loads)
+    mine[...] = loads
 
     coarse_start()
     gathered[me] = mine[...]
 
     consts_arrived()
-    lanes2 = lax.broadcasted_iota(jnp.int32, (ny2, depth), 1)
-    chosen2 = lanes2 % 4 == lax.broadcasted_iota(jnp.int32, (ny2, depth), 0) % 4
-
-    def unfold(places, x, row):
+
+    def unpair(places, x, k):
+        near, far = places[2 * x * grp + k], places[(2 * x + 1) * grp + k]
+        lower = slot[:near.shape[0]] < 2
+        return (jnp.where(lower, near, far),
+                jnp.where(lower, pltpu.roll(near, depth - 2, 1), pltpu.roll(far, 2, 1)))
+
+    def unpack_consts(x):
         for k in range(grp):
-            line = places[(x // bx2) * grp + k, pl.ds(row, 1)]
-            g_a[x, k * by2:(k + 1) * by2] = jnp.broadcast_to(line, (by2, depth))
-        return jnp.where(chosen2, g_a[x], 0.0)
-
-    def widen(values):
-        return pair_lanes(pair_lanes(values, 1, add), 2, add)
-
-    def unpack_consts(x):
-        g_coef[x + 1] = widen(unfold(gathered_c, x, x % bx2))
-        part = unfold(gathered_c, x, bx2)
-        spot = lanes2 // (depth // bx2) == x % bx2
-        top = jnp.max(jnp.where(spot, part, 0.0), axis=1, keepdims=True)
-        g_top[x] = jnp.broadcast_to(top, (ny2, depth))
-
-    planes(0, nx2, unpack_consts)
-    level2 = Level(nx2, ny2, depth, 4, *gw)
-    level2.setup(lambda x: g_coef[x + 1], lambda x: g_top[x], 0, nx2)
+            own = pl.ds(k * by2, by2)
+            g_coef[x + 1, own], g_top[x, own] = unpair(gathered_c, x, k)
+
+    nq = nx2 // 4
+    planes(0, nq, unpack_consts)
+    level2 = Coarse(nq, ny2, depth, *gw)
+    level2.setup(g_coef, g_top)
+    zero = jnp.zeros((ny2, depth), jnp.float32)
+
+    def reset(x):
+        g_p[x] = zero
+        g_s[x] = zero
+        sol[x + 1] = zero
+
+    planes(0, nq, reset)
 
     all_directions(copy_outer, -1, lambda c: c.wait_recv())
 
@@ -432,63 +484,56 @@
 
     coarse_arrived()
 
-    def unpack2(x):
-        load = widen(unfold(gathered, x, x % bx2))
-        g_r[x] = load
-        g_d[x + 1] = load
-
-    planes(0, nx2, unpack2)
-    zero = jnp.zeros((ny2, depth), jnp.float32)
+    def unpack_loads(x):
+        for k in range(grp):
+            low, high = unpair(gathered, x, k)
+            g_r[x + 1, k * by2:k * by2 + rows] = low
+            g_r[x + 1, k * by2 + rows:(k + 1) * by2] = high
+
+    planes(0, nq, unpack_loads)
 
     def total(values):
         return jnp.sum(values, axis=(0, 1), keepdims=True)
 
-    current = total(planes(0, nx2, lambda x, acc: acc + g_r[x] * g_r[x], zero))
-    sol = spread[1]
-
-    def first_sol(x):
-        sol[x] = zero
-
-    planes(0, nx2, first_sol)
-
-    def iterate(_, current):
-        def image(x, acc):
-            applied = level2.apply(g_d, x)
+    def iterate(_, carry):
+        before, step_before = carry
+
+        def image(x, sums):
+            here, applied = level2.apply(g_r, x)
             g_a[x] = applied
-            return acc + g_d[x + 1] * applied
-
-        step = current / total(planes(0, nx2, image, zero))
-
-        def move(x, acc):
-            sol[x] = sol[x] + step * g_d[x + 1]
-            residual = g_r[x] - step * g_a[x]
-            g_r[x] = residual
-            return acc + residual * residual
-
-        following = total(planes(0, nx2, move, zero))
-        ratio = following / current
-
-        def turn(x):
-            g_d[x + 1] = g_r[x] + ratio * g_d[x + 1]
-
-        planes(0, nx2, turn)
-        return following
-
-    lax.fori_loop(0, ITERS, iterate, current)
-
-    pad = 3
-
-    def cut(x):
+            return sums[0] + here * here, sums[1] + here * applied
+
+        squares, products = planes(0, nq, image, (zero, zero))
+        current, curvature = total(squares), total(products)
+        ratio = current / before
+        step = current / (curvature - ratio * current / step_before)
+
+        def move(x):
+            direction = g_r[x + 1] + ratio * g_p[x]
+            applied = g_a[x] + ratio * g_s[x]
+            g_p[x], g_s[x] = direction, applied
+            sol[x + 1] = sol[x + 1] + step * direction
+            g_r[x + 1] = g_r[x + 1] - step * applied
+
+        planes(0, nq, move)
+        return current, step
+
+    one = jnp.ones((1, 1), jnp.float32)
+    lax.fori_loop(0, ITERS, iterate, (one * jnp.inf, one))
+
+    spans = range((2 - ring) // 2, (xo - 3 - ring) // 2 + 1)
+    slot2 = level2.slot
+    for p in spans:
+        x = w * bx2 + p + 4
+        kept = jnp.where(slot2 == lax.rem(x, 4), sol[x // 4], 0.0)
+        kept = pair_lanes(pair_lanes(kept, 1, add), 2, add)
         for k in range(grp):
-            g_x[x + pad, k + 1] = sol[x, k * by2:(k + 1) * by2]
-
-    planes(0, nx2, cut)
-
-    wide_rows = spread[0]
+            g_x[p - spans[0], k + 1] = kept[k * by2:(k + 1) * by2]
+
     for x in range(2, xo - 2):
         parent = (x - ring) // 2
         for k in range(3):
-            piece = g_x[w * bx2 + parent + pad, g + k]
+            piece = g_x[parent - spans[0], g + k]
             wide_rows[x, pl.ds(k * by1, by2, stride=2)] = piece
             wide_rows[x, pl.ds(k * by1 + 1, by2, stride=2)] = piece
         o_corr[x + 1] = o_smooth[x + 1] + level_o.act[x] * wide_rows[x]
@@ -498,7 +543,6 @@
 
     level_o.smooth_again(o_corr, o_load, o_e, o_u, ring - 1, ring + bx1 + 1, put_outer)
 
-    fine_rows = spread[2]
     for x in range(HALO - 2, HALO + bx + 2):
         parent = o_load[(x - HALO) // 2 + ring, by1 - half:2 * by1 + half]
         fine_rows[x, pl.ds(0, y1, stride=2)] = parent
@@ -524,7 +568,7 @@
     x1, y1 = x0 // 2, y0 // 2
     ring = bx1 + 1
     xo, yo = bx1 + 2 * ring, 3 * by1
-    nx2, ny2 = wide * bx2, grp * by2
+    nq, ny2 = wide * bx2 // 4, grp * by2
     peers = wide * grp
 
     def block(*shape):
@@ -541,11 +585,12 @@
         block(x1 + 2, y1), block(bx1 + 2, by1),
         block(xo, yo), block(xo, yo), block(xo + 2, yo), block(xo, yo), held(xo, yo),
         block(xo + 2, yo), block(xo + 2, yo), block(xo, yo), block(xo + 2, yo),
-        block(bx2, y1), block(bx1, by), block(bx2, by1), block(bx2), block(bx2 + 1),
-        block(peers, bx2), block(peers, bx2 + 1),
-        block(nx2 + 2, ny2), block(nx2, ny2), held(nx2, ny2),
-        block(nx2 + 6, grp + 2, by2), block(nx2, ny2), block(nx2 + 2, ny2), block(nx2, ny2),
-        [block(xo, yo), block(nx2, ny2), block(x0, y0)],
+        block(bx2, y1), block(bx1, by), block(bx2, by1), block(by2 // 2), block(by2),
+        block(peers, by2 // 2), block(peers, by2),
+        block(nq + 2, ny2), block(nq, ny2), [block(nq, ny2) for _ in range(8)],
+        block(xo // 2, grp + 2, by2), block(nq + 2, ny2), block(nq, ny2), block(nq, ny2),
+        block(nq, ny2), block(nq + 2, ny2),
+        block(xo, yo), block(x0, y0),
         block(9, bx), pltpu.VMEM((bx, by), jnp.int32), dma((3,)),
         *[dma((8,)) for _ in range(8)], *[dma((peers,)) for _ in range(4)],
     ]
@@ -563,7 +608,7 @@
         out_specs=vmem,
         scratch_shapes=leaves,
         compiler_params=pltpu.CompilerParams(
-            collective_id=0, has_side_effects=True, vmem_limit_bytes=48 * 1024 * 1024
+            collective_id=0, has_side_effects=True, vmem_limit_bytes=64 * 1024 * 1024
         ),
     )(source, conductivity, ice_cells)
 

time: 28.4 us -> 26.3 us (0.926)
  local copies, waits for them, and re-layouts: 3 us -> 1.47 us
  Pallas kernels: 25.2 us -> 24.6 us
    unnamed x7 -> x1, local copies, waits for them, and re-layouts: 3 us -> 1.47 us
    pallas_call x1, Pallas kernels: 25.2 us -> 24.6 us  [shards(): pl.pallas_call(body, out_shape=jax.ShapeDtypeStruct(source.shape, source....]
where the time goes in v3:
time: 26.3 us; the launch traced here: 26.1 us
  Pallas kernels  24.6 us (94%)
  local copies, waits for them, and re-layouts  1.47 us (6%)
    pallas_call x1, Pallas kernels, shards(): pl.pallas_call(body, out_shape=jax.ShapeDtypeStruct(source.shape, source....  24.6 us
    unnamed x1, local copies, waits for them, and re-layouts  1.47 us

profile of v3, /device:TPU:0, one launch (start us, length us, event | category | flops | bytes accessed | tf_op | source)
XLA Modules:
  0.0 26.1 jit_solution(6041200976751439243)
XLA Ops:
  0.0 24.6 %shard_map.37 = f32[8,16,128]{2,1,0:T(8,128)} custom-call(f32[8,16,128]{2,1,0:T(8,128)} %source_ref.1, f32[8,16,128]{2,1,0:T(8,128)} %conductivity_ref.1, s32[8,16]{1,0:T(8,128)} %ice_ref.1), custom_call_target="tpu_custom_call" | custom-call | tf_op jit(solution)/shard_map/pallas_call | solution.py:604
  24.6 1.5 %copy.5 = f32[8,16,128]{2,1,0:T(8,128)} copy(f32[8,16,128]{2,1,0:T(8,128)} %shard_map.37) | data formatting | bytes 131072

commit v4 on v3

--- a/solution.py
+++ b/solution.py
@@ -210,7 +210,7 @@
      outer, o_load, o_coef, o_top, ow, o_u, o_smooth, o_e, o_corr,
      pool_d, pool_g, pool_h, mine, mine_c, gathered, gathered_c,
      g_coef, g_top, gw, g_x, g_r, g_p, g_s, g_a, sol,
-     wide_rows, fine_rows, tops, ice_here, sem_in,
+     wide_rows, fine_rows, tops, ice_here, result, sem_in, sem_out,
      send_a, recv_a, send_t, recv_t, send_s, recv_s, send_b, recv_b,
      send_c, recv_c, send_g, recv_g) = scratch
     bx, by, depth = source.shape
@@ -270,6 +270,88 @@
     load_ice.wait()
     tops[4, :, 0:by] = ice_here[...].astype(jnp.float32)
     load_coef.wait()
+    pl.semaphore_wait(barrier, peers - 1)
+
+    def inside(dx, dy):
+        return (w + dx >= 0) & (w + dx < wide) & (g + dy >= 0) & (g + dy < grp)
+
+    def remote(src, dst, send, recv, device):
+        return pltpu.make_async_remote_copy(
+            src_ref=src, dst_ref=dst, send_sem=send, recv_sem=recv,
+            device_id=device, device_id_type=pl.DeviceIdType.MESH)
+
+    def copy_fine(channel, send, recv):
+        def make(k, dx, dy):
+            rows = (HALO - 2 if dy == 0 else HALO - 3) + channel
+            src_x, dst_x, len_x = {
+                1: (1 + HALO + bx - rows, 1 + HALO - rows, rows),
+                0: (1 + HALO, 1 + HALO, bx),
+                -1: (1 + HALO, 1 + HALO + bx, rows),
+            }[dx]
+            src_y, dst_y, len_y = {
+                1: (by, 0, HALO), 0: (HALO, HALO, by), -1: (HALO, HALO + by, HALO)
+            }[dy]
+            return remote(
+                fine.at[channel, pl.ds(src_x, len_x), pl.ds(src_y, len_y)],
+                fine.at[channel, pl.ds(dst_x, len_x), pl.ds(dst_y, len_y)],
+                send.at[k], recv.at[k], (w + dx, g + dy))
+
+        return make
+
+    copy_coef = copy_fine(1, send_a, recv_a)
+    copy_source = copy_fine(0, send_s, recv_s)
+
+    def copy_tops(k, dx, dy):
+        return remote(tops.at[4], tops.at[(1 - dx) * 3 + 1 - dy],
+                      send_t.at[k], recv_t.at[k], (w + dx, g + dy))
+
+    def copy_outer(k, dx, dy):
+        src_x, dst_x, len_x = {
+            1: (0, 0, ring), 0: (1, ring, bx1), -1: (1, ring + bx1, ring)
+        }[dx]
+        dst_y = {1: 0, 0: by1, -1: 2 * by1}[dy]
+        return remote(packed.at[pl.ds(src_x, len_x)],
+                      outer.at[pl.ds(dst_x, len_x), pl.ds(dst_y, by1)],
+                      send_b.at[k], recv_b.at[k], (w + dx, g + dy))
+
+    def all_directions(make, sign, act):
+        for k, (dx, dy) in enumerate(DIRECTIONS):
+            @pl.when(inside(sign * dx, sign * dy))
+            def _():
+                act(make(k, dx, dy))
+
+    def copy_all(block, places, send, recv):
+        def make(d, owner, to):
+            return remote(block, places.at[owner], send.at[d], recv.at[d], mesh_id(to))
+
+        def start():
+            def body(d, _):
+                make(d, me, lax.rem(me + d, peers)).start()
+                return 0
+            lax.fori_loop(1, peers, body, 0)
+
+        def arrived():
+            def body(d, _):
+                make(d, lax.rem(me + peers - d, peers), me).wait_recv()
+                return 0
+            lax.fori_loop(1, peers, body, 0)
+
+        def sent():
+            def body(d, _):
+                make(d, me, lax.rem(me + d, peers)).wait_send()
+                return 0
+            lax.fori_loop(1, peers, body, 0)
+
+        return start, arrived, sent
+
+    coarse_start, coarse_arrived, coarse_sent = copy_all(mine, gathered, send_c, recv_c)
+    consts_start, consts_arrived, consts_sent = copy_all(mine_c, gathered_c, send_g, recv_g)
+
+    all_directions(copy_coef, 1, lambda c: c.start())
+    all_directions(copy_tops, 1, lambda c: c.start())
+    load_source.wait()
+    all_directions(copy_source, 1, lambda c: c.start())
+
     slot = lax.broadcasted_iota(jnp.int32, (by2, depth), 1) % 4
     pick2 = selector(by2, 0, 4, depth)
     first_slot = lax.rem(w * bx2, 4)
@@ -289,88 +371,6 @@
         consts = jnp.where(slot == here, coef, consts)
         consts = jnp.where(slot == lax.rem(here + 2, 4), column(pick2, top), consts)
     mine_c[...] = consts
-
-    load_source.wait()
-    pl.semaphore_wait(barrier, peers - 1)
-
-    def inside(dx, dy):
-        return (w + dx >= 0) & (w + dx < wide) & (g + dy >= 0) & (g + dy < grp)
-
-    def remote(src, dst, send, recv, device):
-        return pltpu.make_async_remote_copy(
-            src_ref=src, dst_ref=dst, send_sem=send, recv_sem=recv,
-            device_id=device, device_id_type=pl.DeviceIdType.MESH)
-
-    def copy_fine(channel, send, recv):
-        def make(k, dx, dy):
-            rows = (HALO - 2 if dy == 0 else HALO - 3) + channel
-            src_x, dst_x, len_x = {
-                1: (1 + HALO + bx - rows, 1 + HALO - rows, rows),
-                0: (1 + HALO, 1 + HALO, bx),
-                -1: (1 + HALO, 1 + HALO + bx, rows),
-            }[dx]
-            src_y, dst_y, len_y = {
-                1: (by, 0, HALO), 0: (HALO, HALO, by), -1: (HALO, HALO + by, HALO)
-            }[dy]
-            return remote(
-                fine.at[channel, pl.ds(src_x, len_x), pl.ds(src_y, len_y)],
-                fine.at[channel, pl.ds(dst_x, len_x), pl.ds(dst_y, len_y)],
-                send.at[k], recv.at[k], (w + dx, g + dy))
-
-        return make
-
-    copy_coef = copy_fine(1, send_a, recv_a)
-    copy_source = copy_fine(0, send_s, recv_s)
-
-    def copy_tops(k, dx, dy):
-        return remote(tops.at[4], tops.at[(1 - dx) * 3 + 1 - dy],
-                      send_t.at[k], recv_t.at[k], (w + dx, g + dy))
-
-    def copy_outer(k, dx, dy):
-        src_x, dst_x, len_x = {
-            1: (0, 0, ring), 0: (1, ring, bx1), -1: (1, ring + bx1, ring)
-        }[dx]
-        dst_y = {1: 0, 0: by1, -1: 2 * by1}[dy]
-        return remote(packed.at[pl.ds(src_x, len_x)],
-                      outer.at[pl.ds(dst_x, len_x), pl.ds(dst_y, by1)],
-                      send_b.at[k], recv_b.at[k], (w + dx, g + dy))
-
-    def all_directions(make, sign, act):
-        for k, (dx, dy) in enumerate(DIRECTIONS):
-            @pl.when(inside(sign * dx, sign * dy))
-            def _():
-                act(make(k, dx, dy))
-
-    def copy_all(block, places, send, recv):
-        def make(d, owner, to):
-            return remote(block, places.at[owner], send.at[d], recv.at[d], mesh_id(to))
-
-        def start():
-            def body(d, _):
-                make(d, me, lax.rem(me + d, peers)).start()
-                return 0
-            lax.fori_loop(1, peers, body, 0)
-
-        def arrived():
-            def body(d, _):
-                make(d, lax.rem(me + peers - d, peers), me).wait_recv()
-                return 0
-            lax.fori_loop(1, peers, body, 0)
-
-        def sent():
-            def body(d, _):
-                make(d, me, lax.rem(me + d, peers)).wait_send()
-                return 0
-            lax.fori_loop(1, peers, body, 0)
-
-        return start, arrived, sent
-
-    coarse_start, coarse_arrived, coarse_sent = copy_all(mine, gathered, send_c, recv_c)
-    consts_start, consts_arrived, consts_sent = copy_all(mine_c, gathered_c, send_g, recv_g)
-
-    all_directions(copy_coef, 1, lambda c: c.start())
-    all_directions(copy_tops, 1, lambda c: c.start())
-    all_directions(copy_source, 1, lambda c: c.start())
     consts_start()
     gathered_c[me] = mine_c[...]
 
@@ -549,8 +549,12 @@
         fine_rows[x, pl.ds(1, y1, stride=2)] = parent
         f_smooth[x + 1] = f_smooth[x + 1] + level0.act[x] * fine_rows[x]
 
+    def copy_out(x):
+        return pltpu.make_async_copy(result.at[x], out.at[x], sem_out.at[x])
+
     def put_fine(x, value):
-        out[x - HALO] = value[HALO:HALO + by]
+        result[x - HALO] = value[HALO:HALO + by]
+        copy_out(x - HALO).start()
 
     level0.smooth_again(f_smooth, f_load, f_e, f_u, HALO, HALO + bx, put_fine)
 
@@ -558,6 +562,7 @@
         all_directions(make, 1, lambda c: c.wait_send())
     consts_sent()
     coarse_sent()
+    planes(0, bx, lambda x: copy_out(x).wait())
 
 
 def shards(source, conductivity, ice_cells):
@@ -591,7 +596,7 @@
         block(xo // 2, grp + 2, by2), block(nq + 2, ny2), block(nq, ny2), block(nq, ny2),
         block(nq, ny2), block(nq + 2, ny2),
         block(xo, yo), block(x0, y0),
-        block(9, bx), pltpu.VMEM((bx, by), jnp.int32), dma((3,)),
+        block(9, bx), pltpu.VMEM((bx, by), jnp.int32), block(bx, by), dma((3,)), dma((bx,)),
         *[dma((8,)) for _ in range(8)], *[dma((peers,)) for _ in range(4)],
     ]
     leaves, tree = jax.tree.flatten(scratch)
@@ -600,12 +605,12 @@
         kernel(wide, grp, source_ref, conductivity_ref, ice_ref, out_ref,
                *jax.tree.unflatten(tree, refs))
 
-    vmem = pl.BlockSpec(memory_space=pltpu.VMEM)
+    hbm = pl.BlockSpec(memory_space=pltpu.HBM)
     return pl.pallas_call(
         body,
         out_shape=jax.ShapeDtypeStruct(source.shape, source.dtype),
-        in_specs=[pl.BlockSpec(memory_space=pltpu.HBM)] * 3,
-        out_specs=vmem,
+        in_specs=[hbm] * 3,
+        out_specs=hbm,
         scratch_shapes=leaves,
         compiler_params=pltpu.CompilerParams(
             collective_id=0, has_side_effects=True, vmem_limit_bytes=64 * 1024 * 1024

time: 26.3 us -> 25.8 us (0.981)
  Pallas kernels: 24.6 us -> 24.1 us
    pallas_call x1, Pallas kernels: 24.6 us -> 24.1 us  [shards(): pl.pallas_call(body, out_shape=jax.ShapeDtypeStruct(source.shape, source....]
where the time goes in v4:
time: 25.8 us; the launch traced here: 25.6 us
  Pallas kernels  24.1 us (93%)
  local copies, waits for them, and re-layouts  1.47 us (6%)
    pallas_call x1, Pallas kernels, shards(): pl.pallas_call(body, out_shape=jax.ShapeDtypeStruct(source.shape, source....  24.1 us
    unnamed x1, local copies, waits for them, and re-layouts  1.47 us

profile of v4, /device:TPU:0, one launch (start us, length us, event | category | flops | bytes accessed | tf_op | source)
XLA Modules:
  0.0 25.6 jit_solution(8053933315415721735)
XLA Ops:
  0.0 24.1 %shard_map.37 = f32[8,16,128]{2,1,0:T(8,128)} custom-call(f32[8,16,128]{2,1,0:T(8,128)} %source_ref.1, f32[8,16,128]{2,1,0:T(8,128)} %conductivity_ref.1, s32[8,16]{1,0:T(8,128)} %ice_ref.1), custom_call_target="tpu_custom_call" | custom-call | tf_op jit(solution)/shard_map/pallas_call | solution.py:609
  24.1 1.5 %copy.5 = f32[8,16,128]{2,1,0:T(8,128)} copy(f32[8,16,128]{2,1,0:T(8,128)} %shard_map.37) | data formatting | bytes 131072
